TPU v7x, 32 devices: a whole 2x2x4 slice. The times are simulated.
32 devices in a mesh: groups: 2 (over y), down: 4 (over z), cross: 2 (over x), depth: 2 (over core).
Axes of the slice: x: 2, y: 2, z: 4, core: 2. Of those that a mesh axis runs over, the one named last changes fastest.
Arguments:
- positions: float32 [3, 16, 4, 4, 128], P(None, ('groups', 'down'), 'cross', 'depth'), parts along dimension 1, may hold values from -0.5 to 0.5
- velocities: float32 [3, 16, 4, 4, 128], P(None, ('groups', 'down'), 'cross', 'depth'), parts along dimension 1, may hold values from -6 to 6
- sphere_radii: float32 [16, 4, 4, 128], P(('groups', 'down'), 'cross', 'depth'), parts along dimension 0, may hold values from 0.08 to 0.12
- counts: int32 [16, 4, 4], P(('groups', 'down'), 'cross', 'depth'), parts along dimension 0, may hold values from 32 to 128, as said below
- coefficients: float32 [48], replicated, may hold values from -0.6 to 0.6
Outputs:
- velocity_new: float32 [3, 16, 4, 4, 128], P(None, ('groups', 'down'), 'cross', 'depth'), parts along dimension 1
- contact_force: float32 [3, 16, 4, 4, 128], P(None, ('groups', 'down'), 'cross', 'depth'), parts along dimension 1
- residual_field: float32 [16, 4, 4], P(('groups', 'down'), 'cross', 'depth'), parts along dimension 0
- gram_matrix: float32 [96, 48], P('groups'), parts along dimension 0
- moment_vector: float32 [96], P('groups'), parts along dimension 0
There are 2 independent parts, one for each index of `groups`. A program takes and returns all parts, laid end to end along the dimension named above; an argument that names none is the same for every part. Nothing has to cross between parts.
Inputs may be any that keep to these rules, and one draw needn't show every extreme that they name: `counts`: slots 0 to count - 1 of a cell hold spheres, the rest are padding; every cell of the bottom depth layer holds 128.
All inputs are finite; a program needn't handle non-finite values.
Results may differ from a plain program's by a relative error of at most 0.0003.
Values sent between devices are 32-bit elements; how exact they have to be, the bound alone decides.
No kernel may reach another device: no remote copies, remote signals or barrier semaphores. Data moves between devices by JAX's collectives and lax.ppermute only.
A program may use at most 128 MiB of HBM per device.

v0:
```python
import functools

import jax
import jax.numpy as jnp
from jax import lax
from jax.experimental import pallas as pl
from jax.experimental.pallas import tpu as pltpu
from jax.sharding import PartitionSpec as P

STIFFNESS = 100.0
DAMPING = 20.0
TIME_STEP = 0.05
KERNEL_WIDTH = 0.4
KERNEL_NORM = 64.0
SOFTENING = 0.0001
RADIUS_REF = 0.1
MASS_SHIFT = 0.1
DEAD = -1000.0
TERMS = 48
S = 128
SPREAD = 4
F32 = jnp.float32
BF16 = jnp.bfloat16
CELLS = tuple((a, b, z) for a in range(2) for b in range(2) for z in range(2))
PAIR_LIST = ((0, 0), (0, 1), (0, 2), (1, 1), (1, 2), (2, 2))
VMEM_SPEC = pl.BlockSpec(memory_space=pltpu.VMEM)
SMEM_SPEC = pl.BlockSpec(memory_space=pltpu.SMEM)
VMEM_LIMIT = 48 * 1024 * 1024


def row_ids(shape):
    return lax.broadcasted_iota(jnp.int32, shape, 0)


def lane_ids(shape):
    return lax.broadcasted_iota(jnp.int32, shape, 1)


def one_hot(condition):
    return jnp.where(condition, 1.0, 0.0).astype(BF16)


def split(value):
    high = value.astype(BF16)
    return high, value - high.astype(F32)


def matmul(left, right):
    return lax.dot_general(left, right, (((1,), (0,)), ((), ())), preferred_element_type=F32)


def matmul_turned(left, right):
    return lax.dot_general(left, right, (((1,), (1,)), ((), ())), preferred_element_type=F32)


def lane_gather(table, index):
    return jnp.take_along_axis(table, index, axis=1)


def pack_kernel(
    counts_hbm, positions_hbm, velocities_hbm, radii_hbm, own, inner, counts, positions, velocities, radii, arrived
):
    copies = [
        pltpu.make_async_copy(source, target, arrived.at[k])
        for k, (source, target) in enumerate(
            (
                (counts_hbm, counts),
                (positions_hbm, positions),
                (velocities_hbm, velocities),
                (radii_hbm, radii),
            )
        )
    ]
    for copy in copies:
        copy.start()
    for copy in copies:
        copy.wait()
    depth = lax.axis_index("depth")
    lanes = lane_ids((1, S))

    def layer(ref, at, z):
        rows = ref[at]
        return jnp.where(depth == z, rows[0:1], rows[1:2])

    for c, (a, b, z) in enumerate(CELLS):
        for k in range(3):
            own[c * 8 + k : c * 8 + k + 1, :] = layer(positions, (k, a, b), z)
            own[c * 8 + 3 + k : c * 8 + 4 + k, :] = layer(velocities, (k, a, b), z)
        count = jnp.where(depth == z, counts[a, b, 0], counts[a, b, 1])
        own[c * 8 + 6 : c * 8 + 7, :] = jnp.where(lanes < count, layer(radii, (a, b), z), DEAD)
        own[c * 8 + 7 : c * 8 + 8, :] = jnp.zeros((1, S), F32)
    for column in range(4):
        inner[column * 8 : column * 8 + 8, :] = own[column * 16 + 8 : column * 16 + 16, :]


def local_state(raw, centre):
    rows = row_ids(raw.shape)
    shift = jnp.where(rows == 0, centre[0], jnp.where(rows == 1, centre[1], centre[2]))
    return jnp.where(rows < 3, raw + shift, raw)


def plane_reader(refs, height):
    own, depth_halo, sides = refs[0], refs[1], refs[2:]

    def read(ref, cell):
        return ref[cell * height : cell * height + height, :]

    def cell(x, y, slot):
        a = x - 1
        if y in (1, 2):
            return read(own, a * 4 + (y - 1) * 2 + slot) if slot < 2 else read(depth_halo, a * 2 + y - 1)
        if len(sides) == 4:
            before, after, diag_before, diag_after = sides
            if slot < 2:
                return read(before if y == 0 else after, a * 2 + slot)
            return read(diag_before if y == 0 else diag_after, a)
        b = 1 if y == 0 else 0
        return read(sides[0], a * 4 + b * 2 + slot if slot < 2 else 8 + a * 2 + b)

    return cell


def down_reader(refs, height):
    even = lax.rem(lax.axis_index("down"), 2) == 0
    swapped = lax.axis_size("down") % 2 == 0

    def cell(x, y, slot):
        if y in (1, 2):
            place = (y - 1) * 2 + slot if slot < 2 else 4 + y - 1
        else:
            side = 0 if y == 0 else 1
            place = 6 + side * 2 + slot if slot < 2 else 10 + side
        one, two = (ref[place * height : place * height + height, :] for ref in refs)
        if swapped:
            return jnp.where(even, two, one) if x == 0 else jnp.where(even, one, two)
        return one if x == 0 else two

    return cell


def centre_of(x, y, slot, depth):
    side = 0.5 - depth.astype(F32)
    return (x - 1.5, y - 1.5, (-1.0, 1.0, 3.0)[slot] * side)


def extended_cells(xs, depth):
    for k, x in enumerate(xs):
        for y in range(4):
            for slot in range(3):
                yield x, y, slot, ((k * 4 + y) * 3 + slot) * 8, centre_of(x, y, slot, depth)


def stepped_state(old, speed, centre):
    rows = row_ids((3, S))
    shift = jnp.where(rows == 0, centre[0], jnp.where(rows == 1, centre[1], centre[2]))
    return (old[0:3] + TIME_STEP * speed[0:3]) + shift, speed[0:3], old[6:8]


def contact_scratch(width):
    return [
        pltpu.VMEM((24 * 8, S), F32),
        pltpu.VMEM((8 * 8, S), F32),
        pltpu.VMEM((8 * 24, S), jnp.int32),
        pltpu.VMEM((8 * 24, S), jnp.int32),
        pltpu.VMEM((8 * 24, S), jnp.int32),
        pltpu.VMEM((8 * 24, S), jnp.int32),
        pltpu.VMEM((18 * 8 * S, 32), F32),
        pltpu.VMEM((width * 8 * 8, S), F32),
    ]


def contact_sums(xs, width, scratch):
    local_ref, mine_ref, index_ref, base_ref, amount_ref, chosen_ref, list_ref, sum_ref = scratch
    together = xs[1] - xs[0] == 1
    span = 24 if together else 16

    def first_row(a):
        return 0 if together or a == 0 else 8

    def beside(a, b, z):
        return [
            (k * 4 + y) * 3 + slot
            for k, x in enumerate(xs)
            if abs(x - 1 - a) <= 1
            for y in range(b, b + 3)
            for slot in range(3 if z == 1 else 2)
        ]

    sum_ref[...] = jnp.zeros((width * 64, S), F32)
    place = [local_ref[pl.ds(k, 24, stride=8), :] for k in range(3)]
    radius = local_ref[pl.ds(6, 24, stride=8), :]
    rows = row_ids((24, S))
    row_x = jnp.where(rows < 12, xs[0], xs[1])
    row_y, row_slot = (rows // 3) % 4, rows % 3
    masks = []
    for c, (a, b, z) in enumerate(CELLS):
        mine = mine_ref[c * 8 : c * 8 + 8, :]
        live = mine[6:7] > 0.0
        low = jnp.min(jnp.where(live, mine, 1e9), axis=1, keepdims=True)
        high = jnp.max(jnp.where(live, mine, -1e9), axis=1, keepdims=True)
        part = slice(first_row(a), first_row(a) + span)
        reach = radius[part] + high[6:7]
        near = jnp.logical_and(row_y[part] >= b, row_y[part] <= b + 2)
        if not together:
            near = jnp.logical_and(near, row_x[part] == xs[a])
        if z == 0:
            near = jnp.logical_and(near, row_slot[part] < 2)
        for k in range(3):
            near = jnp.logical_and(near, place[k][part] + reach > low[k : k + 1])
            near = jnp.logical_and(near, place[k][part] - reach < high[k : k + 1])
        masks.append(jnp.where(near, 1.0, 0.0).astype(F32))
    mask = jnp.concatenate(masks, axis=0).astype(BF16)
    upper = one_hot(row_ids((S, 2 * S)) <= lane_ids((S, 2 * S)))
    sums = matmul(mask, upper)
    prefix, amount = sums[:, :S], sums[:, S:]
    before = one_hot(lane_ids((span, span)) < row_ids((span, span)))
    total = None
    for c in range(8):
        part = amount[c * span : (c + 1) * span]
        base = matmul(before, part.astype(BF16))
        base_ref[c * span : (c + 1) * span, :] = base.astype(jnp.int32)
        count = base[span - 1 : span] + part[span - 1 : span]
        total = count if total is None else jnp.maximum(total, count)
    most = total.astype(jnp.int32)[0, 0]
    amount_ref[0 : 8 * span, :] = amount.astype(jnp.int32)
    wanted = lane_ids((8 * span, S)).astype(F32)
    index = jnp.zeros((8 * span, S), jnp.int32)
    for step in (64, 32, 16, 8, 4, 2, 1):
        probe = lane_gather(prefix, index + (step - 1))
        index = jnp.where(probe <= wanted, index + step, index)
    index_ref[0 : 8 * span, :] = index
    empty = jnp.where(row_ids((8, S)) == 6, DEAD, 0.0).astype(F32)

    def gather_tiles(t, carry):
        want = t * S + lane_ids((8 * span, S)) - base_ref[0 : 8 * span, :]
        valid = jnp.logical_and(want >= 0, want < amount_ref[0 : 8 * span, :])
        source = lane_gather(index_ref[0 : 8 * span, :], jnp.clip(want, 0, S - 1))
        chosen_ref[0 : 8 * span, :] = jnp.where(valid, source, -1)
        for c, (a, b, z) in enumerate(CELLS):
            tile = empty
            for n in beside(a, b, z):
                row = c * span + n - first_row(a)
                pick = jnp.broadcast_to(chosen_ref[row : row + 1, :], (8, S))
                values = lane_gather(local_ref[n * 8 : n * 8 + 8, :], jnp.maximum(pick, 0))
                tile = jnp.where(pick >= 0, values, tile)
            high = tile.astype(BF16).astype(F32)
            rest = tile - high
            middle = rest.astype(BF16).astype(F32)
            turned = jnp.transpose(jnp.concatenate([high, middle, rest - middle, tile], axis=0))
            for part in range(4):
                start = pl.multiple_of(t * (8 * S) + (part * 8 + c) * 32, 32)
                list_ref[pl.ds(start, 32), :] = turned[part * 32 : part * 32 + 32]
        return carry

    gather_tiles(0, 0)
    lax.fori_loop(1, (most + (S - 1)) // S, gather_tiles, 0)

    selector = jnp.logical_and(
        row_ids((32, SPREAD * S)) % 8 == lane_ids((32, SPREAD * S)) // S, row_ids((32, SPREAD * S)) < 24
    )
    selector = one_hot(selector)

    def pair_step(step, carry):
        every = list_ref[pl.ds(pl.multiple_of(step * 256, 256), 256), :]
        spread = matmul(every.astype(BF16), selector)
        for c in range(8):
            listed = every[c * 32 : c * 32 + 32]
            me = [jnp.broadcast_to(mine_ref[c * 8 + k : c * 8 + k + 1, :], (8, S)) for k in range(7)]
            added = [None] * width
            for block in range(4):
                row = c * 32 + block * 8
                other = [spread[row : row + 8, k * S : (k + 1) * S] for k in range(SPREAD)]
                other += [
                    jnp.broadcast_to(listed[block * 8 : block * 8 + 8, 24 + k : 25 + k], (8, S))
                    for k in range(SPREAD, 7)
                ]
                r = [me[k] - other[k] for k in range(3)]
                u = [me[3 + k] - other[3 + k] for k in range(3)]
                squared = r[0] * r[0] + r[1] * r[1] + r[2] * r[2] + SOFTENING
                inverse = lax.rsqrt(squared)
                along = u[0] * r[0] + u[1] * r[1] + u[2] * r[2]
                overlap = jnp.maximum((me[6] + other[6]) * inverse - 1.0, 0.0)
                weight = overlap * (STIFFNESS - (DAMPING * along) * inverse)
                terms = [weight * r[k] for k in range(3)]
                if width == 9:
                    terms += [terms[left] * r[right] for left, right in PAIR_LIST]
                added = [
                    term if total is None else total + term for total, term in zip(added, terms)
                ]
            for k in range(width):
                row = (k * 8 + c) * 8
                sum_ref[row : row + 8, :] += added[k]
        return carry

    lax.fori_loop(0, (most + 31) // 32, pair_step, 0)
    out = []
    for k in range(width):
        parts = [sum_ref[pl.ds(k * 64 + sub, 8, stride=8), :] for sub in range(8)]
        while len(parts) > 1:
            parts = [parts[i] + parts[i + 1] for i in range(0, len(parts), 2)]
        out.append(parts[0])
    return jnp.concatenate(out, axis=0)


def mass_of(radius):
    scaled = radius / RADIUS_REF
    return scaled * scaled * scaled


def step_inside(*refs):
    pieces, sums_out, scratch = refs[:-9], refs[-9], refs[-8:]
    depth = lax.axis_index("depth")
    cell = plane_reader(pieces, 8)
    for x, y, slot, start, centre in extended_cells((1, 2), depth):
        scratch[0][start : start + 8, :] = local_state(cell(x, y, slot), centre)
    for c, (a, b, z) in enumerate(CELLS):
        start = ((a * 4 + b + 1) * 3 + z) * 8
        scratch[1][c * 8 : c * 8 + 8, :] = scratch[0][start : start + 8, :]
    sums_out[...] = contact_sums((1, 2), 3, scratch)


def step_outside(own, sums_in, near, far, own_out, inner_out, *scratch):
    depth = lax.axis_index("depth")
    cell = down_reader((near, far), 8)
    for x, y, slot, start, centre in extended_cells((0, 3), depth):
        scratch[0][start : start + 8, :] = local_state(cell(x, y, slot), centre)
    for c, (a, b, z) in enumerate(CELLS):
        scratch[1][c * 8 : c * 8 + 8, :] = local_state(
            own[c * 8 : c * 8 + 8, :], centre_of(a + 1, b + 1, z, depth)
        )
    sums = sums_in[...] + contact_sums((0, 3), 3, scratch)
    radius = own[pl.ds(6, 8, stride=8), :]
    safe_mass = jnp.where(radius > 0.0, mass_of(radius), 1.0)
    for k in range(3):
        velocity = own[pl.ds(3 + k, 8, stride=8), :] + TIME_STEP * sums[k * 8 : k * 8 + 8] / safe_mass
        for c in range(8):
            own_out[c * 4 + k : c * 4 + k + 1, :] = velocity[c : c + 1]
    for c in range(8):
        own_out[c * 4 + 3 : c * 4 + 4, :] = jnp.zeros((1, S), F32)
    for column in range(4):
        inner_out[column * 4 : column * 4 + 4, :] = own_out[column * 8 + 4 : column * 8 + 8, :]


def place_state(ref, start, state):
    ref[start : start + 3, :] = state[0]
    ref[start + 3 : start + 6, :] = state[1]
    ref[start + 6 : start + 8, :] = state[2]


def field_inside(*refs):
    count = (len(refs) - 9) // 2
    pieces, speeds, sums_out, scratch = refs[:count], refs[count : 2 * count], refs[-9], refs[-8:]
    depth = lax.axis_index("depth")
    cell, speed = plane_reader(pieces, 8), plane_reader(speeds, 4)
    for x, y, slot, start, centre in extended_cells((1, 2), depth):
        place_state(scratch[0], start, stepped_state(cell(x, y, slot), speed(x, y, slot), centre))
    for c, (a, b, z) in enumerate(CELLS):
        start = ((a * 4 + b + 1) * 3 + z) * 8
        scratch[1][c * 8 : c * 8 + 8, :] = scratch[0][start : start + 8, :]
    sums_out[...] = contact_sums((1, 2), 9, scratch)


def field_outside(
    grid, own, own_speed, sums_in, near_old, far_old, near_speed, far_speed, force_out, node_out, moment_ref, *scratch
):
    depth = lax.axis_index("depth")
    down = lax.axis_index("down")
    cross = lax.axis_index("cross")
    mine_ref = scratch[1]
    cell, speed = down_reader((near_old, far_old), 8), down_reader((near_speed, far_speed), 4)
    for x, y, slot, start, centre in extended_cells((0, 3), depth):
        place_state(scratch[0], start, stepped_state(cell(x, y, slot), speed(x, y, slot), centre))
    for c, (a, b, z) in enumerate(CELLS):
        state = stepped_state(
            own[c * 8 : c * 8 + 8, :],
            own_speed[c * 4 : c * 4 + 4, :],
            centre_of(a + 1, b + 1, z, depth),
        )
        place_state(mine_ref, c * 8, state)
    sums = sums_in[...] + contact_sums((0, 3), 9, scratch)
    force_out[...] = sums[0:24]
    radius = own[pl.ds(6, 8, stride=8), :]
    mass = jnp.where(radius > 0.0, mass_of(radius), 0.0)
    moments = [mass] + [mass * own_speed[pl.ds(k, 8, stride=4), :] for k in range(3)]
    moments += [0.5 * sums[k * 8 : k * 8 + 8] for k in range(3, 9)]
    moment_ref[...] = jnp.zeros((16, 8 * S), F32)
    for m, moment in enumerate(moments):
        for c in range(8):
            moment_ref[m : m + 1, c * S : (c + 1) * S] = moment[c : c + 1]
    rows = row_ids((64, S))
    near_x, near_y, near_z = rows // 16 - 1, (rows // 4) % 4 - 1, rows % 4 - 1
    centres = [index.astype(F32) - 0.5 for index in (near_x, near_y, near_z)]
    kernels = []
    for c, (a, b, z) in enumerate(CELLS):
        squared = jnp.zeros((64, S), F32)
        for k in range(3):
            gap = mine_ref[c * 8 + k : c * 8 + k + 1, :] - centres[k]
            squared = squared + gap * gap
        kernel = jnp.exp(squared * (-0.5 / (KERNEL_WIDTH * KERNEL_WIDTH))) / KERNEL_NORM
        beside = jnp.logical_and(
            jnp.logical_and(jnp.abs(near_x - a) <= 1, jnp.abs(near_y - b) <= 1),
            jnp.abs(near_z - jnp.where(depth == z, 0, 1)) <= 1,
        )
        kernels.append(jnp.where(beside, kernel, 0.0))
    kernel_high, kernel_low = split(jnp.concatenate(kernels, axis=1))
    moment_high, moment_low = split(moment_ref[...])
    wide_part = matmul_turned(
        jnp.concatenate([moment_high, moment_low.astype(BF16)], axis=0), kernel_high
    )
    near = wide_part[0:16] + wide_part[16:32] + matmul_turned(moment_high, kernel_low.astype(BF16))
    size_x, size_y, size_z = grid
    nodes = size_x * size_y * size_z
    lanes = lane_ids((64, nodes))
    row = row_ids((64, nodes))
    target_x = (down * 2 + row // 16 - 1 + size_x) % size_x
    target_y = (cross * 2 + (row // 4) % 4 - 1 + size_y) % size_y
    target_z = depth * 2 + row % 4 - 1
    inside = jnp.logical_and(target_z >= 0, target_z < size_z)
    target = (target_x * size_y + target_y) * size_z + target_z
    chosen = one_hot(jnp.logical_and(inside, lanes == target))
    near_high, rest = split(near)
    near_middle, near_low = split(rest)
    placed = matmul(
        jnp.concatenate([near_high, near_middle, near_low.astype(BF16)], axis=0), chosen
    )
    node_out[...] = placed[0:16] + placed[16:32] + placed[32:48]


def library_kernel(
    grid, coefficients, mine, other, speed, force, velocity_out, force_out, residual_out, gram_out, moment_out, terms
):
    flat = lax.axis_index("depth") == 0
    for k in range(3):
        for a in range(2):
            for b in range(2):
                c = a * 4 + b * 2
                layers = [speed[(c + z) * 4 + k : (c + z) * 4 + k + 1, :] for z in range(2)]
                pulls = [force[k * 8 + c + z : k * 8 + c + z + 1, :] for z in range(2)]
                for z in range(2):
                    velocity_out[k, a, b, z : z + 1, :] = jnp.where(flat, layers[z], layers[1 - z])
                    force_out[k, a, b, z : z + 1, :] = jnp.where(flat, pulls[z], pulls[1 - z])
    fields = mine[...] + other[...]
    size_x, size_y, size_z = grid
    nodes = size_x * size_y * size_z
    lanes = lax.broadcasted_iota(jnp.int32, (1, nodes), 1)
    node_x = lanes // (size_y * size_z)
    node_y = (lanes // size_z) % size_y
    node_z = lanes % size_z
    rows = row_ids((8, nodes))
    density = fields[0:1]
    values = jnp.where(rows == 0, fields[0:8], fields[0:8] / (density + MASS_SHIFT))

    def moved(value, step):
        return pltpu.roll(value, step % nodes, 1)

    plane = size_y * size_z
    slope_x = (moved(values, -plane) - moved(values, plane)) * 0.5
    after_y = jnp.where(
        node_y == size_y - 1, moved(values, (size_y - 1) * size_z), moved(values, -size_z)
    )
    before_y = jnp.where(
        node_y == 0, moved(values, -(size_y - 1) * size_z), moved(values, size_z)
    )
    slope_y = (after_y - before_y) * 0.5
    after_z = jnp.where(node_z == size_z - 1, 0.0, moved(values, -1))
    before_z = jnp.where(node_z == 0, 0.0, moved(values, 1))
    slope_z = (after_z - before_z) * 0.5
    slopes = [[table[k : k + 1] for k in range(4)] for table in (slope_x, slope_y, slope_z)]
    strain = [
        [0.5 * (slopes[left][1 + right] + slopes[right][1 + left]) for right in range(3)]
        for left in range(3)
    ]
    divergence = strain[0][0] + strain[1][1] + strain[2][2]
    rate_sum = jnp.zeros_like(density)
    for left in range(3):
        for right in range(3):
            entry = strain[left][right]
            if left == right:
                entry = entry - divergence / 3.0
            rate_sum = rate_sum + entry * entry
    shear_rate = jnp.sqrt(2.0 * rate_sum + 0.01)
    stress = [fields[4 + k : 5 + k] for k in range(6)]
    pressure = (stress[0] + stress[3] + stress[5]) / 3.0
    deviator = (
        (stress[0] - pressure) ** 2
        + (stress[3] - pressure) ** 2
        + (stress[5] - pressure) ** 2
        + 2.0 * (stress[1] ** 2 + stress[2] ** 2 + stress[4] ** 2)
    )
    shear_stress = jnp.sqrt(0.5 * deviator + 0.01)
    pressure_scale = jnp.sqrt(pressure * pressure + 1.0)
    friction = shear_stress / pressure_scale
    features = [
        density,
        pressure / pressure_scale,
        shear_rate,
        shear_rate / jnp.sqrt(pressure_scale),
        divergence,
        slopes[0][0],
        slopes[1][0],
        slopes[2][0],
    ]
    entries = list(features)
    for left in range(8):
        for right in range(left, 8):
            entries.append(features[left] * features[right])
    for left in range(1, 5):
        entries.append(features[left] * features[left] * features[left])
    model = jnp.zeros_like(density)
    for k, entry in enumerate(entries):
        terms[k : k + 1, :] = entry
        model = model + coefficients[k] * entry
    residual = friction - model
    table = terms[...]
    gram_out[...] = (
        lax.dot_general(
            table,
            table,
            (((1,), (1,)), ((), ())),
            precision=lax.Precision.HIGHEST,
            preferred_element_type=F32,
        )
        / nodes
    )
    moment = lax.dot_general(
        jnp.broadcast_to(friction, (8, nodes)),
        table,
        (((1,), (1,)), ((), ())),
        precision=lax.Precision.HIGHEST,
        preferred_element_type=F32,
    )
    moment_out[...] = moment[0:1] / nodes
    down = lax.axis_index("down")
    cross = lax.axis_index("cross")
    depth = lax.axis_index("depth")
    b_rows = lax.broadcasted_iota(jnp.int32, (2, 1), 0)
    z_lanes = lax.broadcasted_iota(jnp.int32, (2, 2), 1)
    for a in range(2):
        mine = jnp.logical_and(node_x == down * 2 + a, node_y == cross * 2 + b_rows)
        column = [
            jnp.sum(
                jnp.where(jnp.logical_and(mine, node_z == depth * 2 + z), residual, 0.0),
                axis=1,
                keepdims=True,
            )
            for z in range(2)
        ]
        residual_out[a] = jnp.where(z_lanes == 0, column[0], column[1])


def ring(axis, step):
    peers = lax.axis_size(axis)
    return [(i, (i + step) % peers) for i in range(peers)]


def exchange(own, inner, height):
    cross = lax.axis_size("cross")

    def cells(block, first, count):
        return block[first * height : (first + count) * height]

    depth_halo = lax.ppermute(inner, "depth", [(0, 1), (1, 0)])
    if cross == 2:
        side = lax.ppermute(
            jnp.concatenate([own, depth_halo], axis=0), "cross", [(0, 1), (1, 0)]
        )
        sides = [side]

        def lateral(x):
            return [
                cells(side, x * 4 + 2, 2),
                cells(side, x * 4, 2),
                cells(side, 8 + x * 2 + 1, 1),
                cells(side, 8 + x * 2, 1),
            ]

    else:
        pairs = [(i * 2 + j, ((i + 1) % cross) * 2 + 1 - j) for i in range(cross) for j in range(2)]
        back = [(i * 2 + j, ((i - 1) % cross) * 2 + 1 - j) for i in range(cross) for j in range(2)]
        last = jnp.concatenate([cells(own, 2, 2), cells(own, 6, 2)], axis=0)
        first = jnp.concatenate([cells(own, 0, 2), cells(own, 4, 2)], axis=0)
        last_inner = jnp.concatenate([cells(inner, 1, 1), cells(inner, 3, 1)], axis=0)
        first_inner = jnp.concatenate([cells(inner, 0, 1), cells(inner, 2, 1)], axis=0)
        before = lax.ppermute(last, "cross", ring("cross", 1))
        after = lax.ppermute(first, "cross", ring("cross", -1))
        diag_before = lax.ppermute(last_inner, ("cross", "depth"), pairs)
        diag_after = lax.ppermute(first_inner, ("cross", "depth"), back)
        sides = [before, after, diag_before, diag_after]

        def lateral(x):
            return [
                cells(before, x * 2, 2),
                cells(after, x * 2, 2),
                cells(diag_before, x, 1),
                cells(diag_after, x, 1),
            ]

    def face(x):
        return jnp.concatenate([cells(own, x * 4, 4), cells(depth_halo, x * 2, 2)] + lateral(x), axis=0)

    downs = lax.axis_size("down")
    last, first = face(1), face(0)
    if downs % 2 == 0:
        even = lax.rem(lax.axis_index("down"), 2) == 0
        near = [(i, i ^ 1) for i in range(downs)]
        far = [(i, (i - 1 + 2 * (i % 2)) % downs) for i in range(downs)]
        outside = [
            lax.ppermute(jnp.where(even, last, first), "down", near),
            lax.ppermute(jnp.where(even, first, last), "down", far),
        ]
    else:
        outside = [
            lax.ppermute(last, "down", ring("down", 1)),
            lax.ppermute(first, "down", ring("down", -1)),
        ]
    return [own, depth_halo] + sides, outside


def shared(value, axes, peers):
    return [value] + [
        lax.ppermute(value, axes, [(i, i ^ k) for i in range(peers)]) for k in range(1, peers)
    ]


def tree_sum(parts):
    while len(parts) > 1:
        parts = [parts[k] + parts[k + 1] for k in range(0, len(parts), 2)]
    return parts[0]


def body(positions, velocities, sphere_radii, counts, coefficients):
    down, cross, depth = (lax.axis_size(name) for name in ("down", "cross", "depth"))
    grid = (2 * down, 2 * cross, 2 * depth)
    nodes = grid[0] * grid[1] * grid[2]
    params = pltpu.CompilerParams(vmem_limit_bytes=VMEM_LIMIT)
    vector_shape = jax.ShapeDtypeStruct((3, 2, 2, 2, S), F32)

    def rows(count):
        return jax.ShapeDtypeStruct((count, S), F32)

    def call(kernel, inputs, outputs, scratch, name, vectors=0):
        return pl.pallas_call(
            kernel,
            out_shape=outputs,
            in_specs=[VMEM_SPEC] * len(inputs),
            out_specs=jax.tree.map(lambda _: VMEM_SPEC, outputs),
            scratch_shapes=scratch,
            compiler_params=params,
            cost_estimate=pl.CostEstimate(flops=vectors, bytes_accessed=1 << 20, transcendentals=0),
            name=name,
        )(*inputs)

    own, inner = pl.pallas_call(
        pack_kernel,
        out_shape=(rows(64), rows(32)),
        in_specs=[pl.BlockSpec(memory_space=pl.ANY)] * 4,
        out_specs=(VMEM_SPEC, VMEM_SPEC),
        scratch_shapes=[
            pltpu.SMEM((2, 2, 2), jnp.int32),
            pltpu.VMEM((3, 2, 2, 2, S), F32),
            pltpu.VMEM((3, 2, 2, 2, S), F32),
            pltpu.VMEM((2, 2, 2, S), F32),
            pltpu.SemaphoreType.DMA((4,)),
        ],
        compiler_params=pltpu.CompilerParams(vmem_limit_bytes=60 * 1024 * 1024),
        name="pack",
    )(counts, positions, velocities, sphere_radii)
    inside, outside = exchange(own, inner, 8)
    sums = call(step_inside, inside, rows(24), contact_scratch(3), "step_inside", 1 << 31)
    own_speed, inner_speed = call(
        step_outside, [own, sums] + outside, (rows(32), rows(16)), contact_scratch(3), "step_outside", 1 << 30
    )
    inside_speed, outside_speed = exchange(own_speed, inner_speed, 4)
    sums = call(
        field_inside, inside + inside_speed, rows(72), contact_scratch(9), "field_inside", 1 << 31
    )
    force, partial = call(
        functools.partial(field_outside, grid),
        [own, own_speed, sums] + outside + outside_speed,
        (rows(24), jax.ShapeDtypeStruct((16, nodes), F32)),
        [pltpu.VMEM((16, 8 * S), F32)] + contact_scratch(9),
        "field_outside",
        1 << 30,
    )
    for axis in ("depth", "cross"):
        partial = tree_sum(shared(partial, axis, lax.axis_size(axis)))
    distance = 1
    while distance < down:
        other = lax.ppermute(partial, "down", [(i, i ^ distance) for i in range(down)])
        distance = distance * 2
        if distance < down:
            partial = partial + other
    velocity_new, force_next, residual_field, gram_matrix, moment = pl.pallas_call(
        functools.partial(library_kernel, grid),
        out_shape=(
            vector_shape,
            vector_shape,
            jax.ShapeDtypeStruct((2, 2, 2), F32),
            jax.ShapeDtypeStruct((TERMS, TERMS), F32),
            jax.ShapeDtypeStruct((1, TERMS), F32),
        ),
        in_specs=[SMEM_SPEC] + [VMEM_SPEC] * 4,
        out_specs=(VMEM_SPEC,) * 5,
        scratch_shapes=[pltpu.VMEM((TERMS, nodes), F32)],
        compiler_params=params,
        name="library",
    )(coefficients, partial, other, own_speed, force)
    return (velocity_new, force_next, residual_field, gram_matrix, moment.reshape(TERMS))


def solution(mesh):
    return jax.shard_map(
        body,
        mesh=mesh,
        in_specs=(
            P(None, ("groups", "down"), "cross", "depth", None),
            P(None, ("groups", "down"), "cross", "depth", None),
            P(("groups", "down"), "cross", "depth", None),
            P(("groups", "down"), "cross", "depth"),
            P(),
        ),
        out_specs=(
            P(None, ("groups", "down"), "cross", "depth", None),
            P(None, ("groups", "down"), "cross", "depth", None),
            P(("groups", "down"), "cross", "depth"),
            P("groups", None),
            P("groups"),
        ),
        check_vma=False,
    )
```

profile of v0, /device:TPU:0, one launch (start us, length us, event | category | flops | bytes accessed | tf_op | source)
XLA Modules:
  0.0 47.4 jit_solution(9773688359511130553)
XLA Ops:
  0.6 1.4 %pack.1 = (f32[64,128]{1,0:T(8,128)}, f32[32,128]{1,0:T(8,128)}) custom-call(s32[2,2,2]{2,1,0:T(2,128)} %counts_hbm.1, f32[3,2,2,2,128]{4,3,2,1,0:T(2,128)} %positions_hbm.1, f32[3,2,2,2,128]{4,3,2,1,0:T(2,128)} %velocities_hbm.1, f32[2,2,2,128]{3,2,1,0:T(2,128)} %radii_hbm.1), custom_call_target="tpu_custom_call" | custom-call | tf_op jit(solution)/shard_map/pack/pallas_call | solution.py:653
  2.0 0.5 %collective-permute-start = (f32[32,128]{1,0:T(8,128)}, f32[32,128]{1,0:T(8,128)S(1)}, u32[]{:S(2)}, u32[]{:S(2)}) collective-permute-start(f32[32,128]{1,0:T(8,128)} %get-tuple-element.17), channel_id=1, source_target_pairs={{0,1},{1,0},{2,3},{3,2},{4,5},{5,4},{6,7},{7,6},{8,9},{9,8},{10,11... | collective-permute-start | bytes 49160 | tf_op jit(solution)/shard_map/ppermute | solution.py:562
  2.6 0.8 %constant_dynamic-update-slice_fusion.11 = (f32[96,128]{1,0:T(8,128)S(1)}, f32[96,128]{1,0:T(8,128)S(1)}) fusion(f32[64,128]{1,0:T(8,128)} %get-tuple-element.16.refs_0_.own), kind=kLoop, calls=%fused_computation.12 | loop fusion | bytes 65536
  3.4 0.3 collective-permute-done.refs_1_
  3.6 0.0 copy-done
  3.6 2.9 %collective-permute-start.1 = (f32[96,128]{1,0:T(8,128)S(1)}, f32[96,128]{1,0:T(8,128)S(1)}, u32[]{:S(2)}, u32[]{:S(2)}) collective-permute-start(f32[96,128]{1,0:T(8,128)S(1)} %pad_maximum_fusion), channel_id=1, source_target_pairs={{0,2},{2,0},{1,3},{3,1},{4,6},{6,4},{5,7},{7,5},{8,10},{10,8},{9,1... | collective-permute-start | bytes 147464 | tf_op jit(solution)/shard_map/ppermute | solution.py:564
  6.5 2.1 %collective-permute-done.1.refs_2_ = f32[96,128]{1,0:T(8,128)S(1)} collective-permute-done((f32[96,128]{1,0:T(8,128)S(1)}, f32[96,128]{1,0:T(8,128)S(1)}, u32[]{:S(2)}, u32[]{:S(2)}) %collective-permute-start.1) | collective-permute-done | bytes 49184 | tf_op jit(solution)/shard_map/ppermute | solution.py:564
  8.6 4.2 %collective-permute-start.3 = (f32[96,128]{1,0:T(8,128)S(1)}, f32[96,128]{1,0:T(8,128)S(1)}, u32[]{:S(2)}, u32[]{:S(2)}) collective-permute-start(f32[96,128]{1,0:T(8,128)S(1)} %get-tuple-element.27), channel_id=1, source_target_pairs={{0,12},{4,8},{8,4},{12,0},{1,13},{5,9},{9,5},{13,1},{2,14},{6,10},... | collective-permute-start | bytes 147464 | tf_op jit(solution)/shard_map/ppermute | solution.py:609
  12.8 0.0 collective-permute-start.2
  12.8 3.4 %step_inside.1.sums_in = f32[24,128]{1,0:T(8,128)S(1)} custom-call(f32[64,128]{1,0:T(8,128)S(1)} %copy-done, f32[32,128]{1,0:T(8,128)S(1)} %collective-permute-done.refs_1_, f32[96,128]{1,0:T(8,128)S(1)} %collective-permute-done.1.refs_2_), custom_call_target="tpu_custom_call" | custom-call | flops 2147483648 | bytes 1048576 | tf_op jit(solution)/shard_map/step_inside/pallas_call | solution.py:642
  16.2 0.0 collective-permute-done.3.far.far_old
  16.2 0.7 %collective-permute-done.2.near.near_old = f32[96,128]{1,0:T(8,128)S(1)} collective-permute-done((f32[96,128]{1,0:T(8,128)S(1)}, f32[96,128]{1,0:T(8,128)S(1)}, u32[]{:S(2)}, u32[]{:S(2)}) %collective-permute-start.2) | collective-permute-done | bytes 49184 | tf_op jit(solution)/shard_map/ppermute | solution.py:608
  16.9 1.6 %step_outside.1 = (f32[32,128]{1,0:T(8,128)S(1)}, f32[16,128]{1,0:T(8,128)S(1)}) custom-call(f32[64,128]{1,0:T(8,128)S(1)} %copy-done, f32[24,128]{1,0:T(8,128)S(1)} %step_inside.1.sums_in, f32[96,128]{1,0:T(8,128)S(1)} %collective-permute-done.2.near.near_old, f32[96,128]{1,0:T(8,128)S(1)} %collective-permute-done.3.far.far_old), custom_call_target="tpu_custom_call" | custom-call | flops 1073741824 | bytes 1048576 | tf_op jit(solution)/shard_map/step_outside/pallas_call | solution.py:642
  18.5 0.1 collective-permute-start.4
  18.5 1.1 %collective-permute-done.4.refs_4_ = f32[16,128]{1,0:T(8,128)S(1)} collective-permute-done((f32[16,128]{1,0:T(8,128)S(1)}, f32[16,128]{1,0:T(8,128)S(1)}, u32[]{:S(2)}, u32[]{:S(2)}) %collective-permute-start.4) | collective-permute-done | bytes 8224 | tf_op jit(solution)/shard_map/ppermute | solution.py:562
  19.7 1.5 %collective-permute-start.5 = (f32[48,128]{1,0:T(8,128)S(1)}, f32[48,128]{1,0:T(8,128)S(1)}, u32[]{:S(2)}, u32[]{:S(2)}) collective-permute-start(f32[48,128]{1,0:T(8,128)S(1)} %pad_maximum_fusion.1), channel_id=1, source_target_pairs={{0,2},{2,0},{1,3},{3,1},{4,6},{6,4},{5,7},{7,5},{8,10},{10,8},{9,1... | collective-permute-start | bytes 73736 | tf_op jit(solution)/shard_map/ppermute | solution.py:564
  21.2 2.3 %collective-permute-done.5.refs_5_ = f32[48,128]{1,0:T(8,128)S(1)} collective-permute-done((f32[48,128]{1,0:T(8,128)S(1)}, f32[48,128]{1,0:T(8,128)S(1)}, u32[]{:S(2)}, u32[]{:S(2)}) %collective-permute-start.5) | collective-permute-done | bytes 24608 | tf_op jit(solution)/shard_map/ppermute | solution.py:564
  23.6 1.9 %collective-permute-start.7 = (f32[48,128]{1,0:T(8,128)S(1)}, f32[48,128]{1,0:T(8,128)S(1)}, u32[]{:S(2)}, u32[]{:S(2)}) collective-permute-start(f32[48,128]{1,0:T(8,128)S(1)} %get-tuple-element.29), channel_id=1, source_target_pairs={{0,12},{4,8},{8,4},{12,0},{1,13},{5,9},{9,5},{13,1},{2,14},{6,10},... | collective-permute-start | bytes 73736 | tf_op jit(solution)/shard_map/ppermute | solution.py:609
  25.5 0.0 collective-permute-start.6
  25.5 4.4 %field_inside.1.sums_in = f32[72,128]{1,0:T(8,128)S(1)} custom-call(f32[64,128]{1,0:T(8,128)S(1)} %copy-done, f32[32,128]{1,0:T(8,128)S(1)} %collective-permute-done.refs_1_, f32[96,128]{1,0:T(8,128)S(1)} %collective-permute-done.1.refs_2_, f32[32,128]{1,0:T(8,128)S(1)} %get-tuple-element.18.refs_3_.own_speed.speed, ...), custom_call_target="tpu_custom_call" | custom-call | flops 2147483648 | bytes 1048576 | tf_op jit(solution)/shard_map/field_inside/pallas_call | solution.py:642
  29.9 0.0 collective-permute-done.7.far_speed
  29.9 0.0 collective-permute-done.6.near_speed
  29.9 2.5 %field_outside.1 = (f32[24,128]{1,0:T(8,128)S(1)}, f32[16,128]{1,0:T(8,128)S(1)}) custom-call(f32[64,128]{1,0:T(8,128)S(1)} %copy-done, f32[32,128]{1,0:T(8,128)S(1)} %get-tuple-element.18.refs_3_.own_speed.speed, f32[72,128]{1,0:T(8,128)S(1)} %field_inside.1.sums_in, f32[96,128]{1,0:T(8,128)S(1)} %collective-permute-done.2.near.near_old, ...), custom_call_target="tpu_custom_call" | custom-call | flops 1073741824 | bytes 1048576 | tf_op jit(solution)/shard_map/field_outside/pallas_call | solution.py:642
  32.4 0.0 collective-permute-start.8
  32.4 1.2 %collective-permute-done.8 = f32[16,128]{1,0:T(8,128)S(1)} collective-permute-done((f32[16,128]{1,0:T(8,128)S(1)}, f32[16,128]{1,0:T(8,128)S(1)}, u32[]{:S(2)}, u32[]{:S(2)}) %collective-permute-start.8) | collective-permute-done | bytes 8224 | tf_op jit(solution)/shard_map/ppermute | solution.py:621
  33.6 2.1 %collective-permute-start.9 = (f32[16,128]{1,0:T(8,128)S(1)}, f32[16,128]{1,0:T(8,128)S(1)}, u32[]{:S(2)}, u32[]{:S(2)}) collective-permute-start(f32[16,128]{1,0:T(8,128)S(1)} %add.9), channel_id=1, source_target_pairs={{0,2},{2,0},{1,3},{3,1},{4,6},{6,4},{5,7},{7,5},{8,10},{10,8},{9,1... | collective-permute-start | bytes 24584 | tf_op jit(solution)/shard_map/ppermute | solution.py:621
  35.7 1.6 %collective-permute-done.9 = f32[16,128]{1,0:T(8,128)S(1)} collective-permute-done((f32[16,128]{1,0:T(8,128)S(1)}, f32[16,128]{1,0:T(8,128)S(1)}, u32[]{:S(2)}, u32[]{:S(2)}) %collective-permute-start.9) | collective-permute-done | bytes 8224 | tf_op jit(solution)/shard_map/ppermute | solution.py:621
  37.4 2.0 %collective-permute-start.10 = (f32[16,128]{1,0:T(8,128)S(1)}, f32[16,128]{1,0:T(8,128)S(1)}, u32[]{:S(2)}, u32[]{:S(2)}) collective-permute-start(f32[16,128]{1,0:T(8,128)S(1)} %add.10), channel_id=1, source_target_pairs={{0,4},{4,0},{8,12},{12,8},{1,5},{5,1},{9,13},{13,9},{2,6},{6,2},{1... | collective-permute-start | bytes 24584 | tf_op jit(solution)/shard_map/ppermute | solution.py:689
  39.4 1.6 %collective-permute-done.10 = f32[16,128]{1,0:T(8,128)S(1)} collective-permute-done((f32[16,128]{1,0:T(8,128)S(1)}, f32[16,128]{1,0:T(8,128)S(1)}, u32[]{:S(2)}, u32[]{:S(2)}) %collective-permute-start.10) | collective-permute-done | bytes 8224 | tf_op jit(solution)/shard_map/ppermute | solution.py:689
  41.0 3.3 %collective-permute-start.11 = (f32[16,128]{1,0:T(8,128)S(1)}, f32[16,128]{1,0:T(8,128)S(1)}, u32[]{:S(2)}, u32[]{:S(2)}) collective-permute-start(f32[16,128]{1,0:T(8,128)S(1)} %add.11.mine), channel_id=1, source_target_pairs={{0,8},{4,12},{8,0},{12,4},{1,9},{5,13},{9,1},{13,5},{2,10},{6,14},... | collective-permute-start | bytes 24584 | tf_op jit(solution)/shard_map/ppermute | solution.py:689
  44.3 1.6 %collective-permute-done.11.other = f32[16,128]{1,0:T(8,128)S(1)} collective-permute-done((f32[16,128]{1,0:T(8,128)S(1)}, f32[16,128]{1,0:T(8,128)S(1)}, u32[]{:S(2)}, u32[]{:S(2)}) %collective-permute-start.11) | collective-permute-done | bytes 8224 | tf_op jit(solution)/shard_map/ppermute | solution.py:689
  45.9 1.5 %library.1 = (f32[3,2,2,2,128]{4,3,2,1,0:T(2,128)}, f32[3,2,2,2,128]{4,3,2,1,0:T(2,128)}, f32[2,2,2]{2,1,0:T(2,128)}, f32[48,48]{1,0:T(8,128)}, f32[1,48]{1,0:T(1,128)}) custom-call(f32[48]{0:T(128)S(1)} %copy-done.1, f32[16,128]{1,0:T(8,128)S(1)} %add.11.mine, f32[16,128]{1,0:T(8,128)S(1)} %collective-permute-done.11.other, ...), custom_call_target="tpu_custom_call" | custom-call | tf_op jit(solution)/shard_map/library/pallas_call | solution.py:693
  (21 shorter events, 0.1 us)
Async XLA Ops:
  2.0 1.6 %collective-permute-start = (f32[32,128]{1,0:T(8,128)}, f32[32,128]{1,0:T(8,128)S(1)}, u32[]{:S(2)}, u32[]{:S(2)}) collective-permute-start(f32[32,128]{1,0:T(8,128)} %get-tuple-element.17), channel_id=1, source_target_pairs={{0,1},{1,0},{2,3},{3,2},{4,5},{5,4},{6,7},{7,6},{8,9},{9,8},{10,11... | collective-permute-start | bytes 49160 | tf_op jit(solution)/shard_map/ppermute | solution.py:562
  2.6 1.1 %copy-start = (f32[64,128]{1,0:T(8,128)S(1)}, f32[64,128]{1,0:T(8,128)}, u32[]{:S(2)}) copy-start(f32[64,128]{1,0:T(8,128)} %get-tuple-element.16.refs_0_.own) | copy-start | bytes 98308
  3.6 5.0 %collective-permute-start.1 = (f32[96,128]{1,0:T(8,128)S(1)}, f32[96,128]{1,0:T(8,128)S(1)}, u32[]{:S(2)}, u32[]{:S(2)}) collective-permute-start(f32[96,128]{1,0:T(8,128)S(1)} %pad_maximum_fusion), channel_id=1, source_target_pairs={{0,2},{2,0},{1,3},{3,1},{4,6},{6,4},{5,7},{7,5},{8,10},{10,8},{9,1... | collective-permute-start | bytes 147464 | tf_op jit(solution)/shard_map/ppermute | solution.py:564
  8.6 7.6 %collective-permute-start.3 = (f32[96,128]{1,0:T(8,128)S(1)}, f32[96,128]{1,0:T(8,128)S(1)}, u32[]{:S(2)}, u32[]{:S(2)}) collective-permute-start(f32[96,128]{1,0:T(8,128)S(1)} %get-tuple-element.27), channel_id=1, source_target_pairs={{0,12},{4,8},{8,4},{12,0},{1,13},{5,9},{9,5},{13,1},{2,14},{6,10},... | collective-permute-start | bytes 147464 | tf_op jit(solution)/shard_map/ppermute | solution.py:609
  12.8 4.1 %collective-permute-start.2 = (f32[96,128]{1,0:T(8,128)S(1)}, f32[96,128]{1,0:T(8,128)S(1)}, u32[]{:S(2)}, u32[]{:S(2)}) collective-permute-start(f32[96,128]{1,0:T(8,128)S(1)} %get-tuple-element.28), channel_id=1, source_target_pairs={{0,4},{4,0},{8,12},{12,8},{1,5},{5,1},{9,13},{13,9},{2,6},{6,2},{1... | collective-permute-start | bytes 147464 | tf_op jit(solution)/shard_map/ppermute | solution.py:608
  18.5 1.2 %collective-permute-start.4 = (f32[16,128]{1,0:T(8,128)S(1)}, f32[16,128]{1,0:T(8,128)S(1)}, u32[]{:S(2)}, u32[]{:S(2)}) collective-permute-start(f32[16,128]{1,0:T(8,128)S(1)} %get-tuple-element.19), channel_id=1, source_target_pairs={{0,1},{1,0},{2,3},{3,2},{4,5},{5,4},{6,7},{7,6},{8,9},{9,8},{10,11... | collective-permute-start | bytes 24584 | tf_op jit(solution)/shard_map/ppermute | solution.py:562
  19.7 3.8 %collective-permute-start.5 = (f32[48,128]{1,0:T(8,128)S(1)}, f32[48,128]{1,0:T(8,128)S(1)}, u32[]{:S(2)}, u32[]{:S(2)}) collective-permute-start(f32[48,128]{1,0:T(8,128)S(1)} %pad_maximum_fusion.1), channel_id=1, source_target_pairs={{0,2},{2,0},{1,3},{3,1},{4,6},{6,4},{5,7},{7,5},{8,10},{10,8},{9,1... | collective-permute-start | bytes 73736 | tf_op jit(solution)/shard_map/ppermute | solution.py:564
  23.6 6.3 %collective-permute-start.7 = (f32[48,128]{1,0:T(8,128)S(1)}, f32[48,128]{1,0:T(8,128)S(1)}, u32[]{:S(2)}, u32[]{:S(2)}) collective-permute-start(f32[48,128]{1,0:T(8,128)S(1)} %get-tuple-element.29), channel_id=1, source_target_pairs={{0,12},{4,8},{8,4},{12,0},{1,13},{5,9},{9,5},{13,1},{2,14},{6,10},... | collective-permute-start | bytes 73736 | tf_op jit(solution)/shard_map/ppermute | solution.py:609
  25.5 4.5 %collective-permute-start.6 = (f32[48,128]{1,0:T(8,128)S(1)}, f32[48,128]{1,0:T(8,128)S(1)}, u32[]{:S(2)}, u32[]{:S(2)}) collective-permute-start(f32[48,128]{1,0:T(8,128)S(1)} %get-tuple-element.30), channel_id=1, source_target_pairs={{0,4},{4,0},{8,12},{12,8},{1,5},{5,1},{9,13},{13,9},{2,6},{6,2},{1... | collective-permute-start | bytes 73736 | tf_op jit(solution)/shard_map/ppermute | solution.py:608
  32.4 1.2 %collective-permute-start.8 = (f32[16,128]{1,0:T(8,128)S(1)}, f32[16,128]{1,0:T(8,128)S(1)}, u32[]{:S(2)}, u32[]{:S(2)}) collective-permute-start(f32[16,128]{1,0:T(8,128)S(1)} %get-tuple-element.20), channel_id=1, source_target_pairs={{0,1},{1,0},{2,3},{3,2},{4,5},{5,4},{6,7},{7,6},{8,9},{9,8},{10,11... | collective-permute-start | bytes 24584 | tf_op jit(solution)/shard_map/ppermute | solution.py:621
  33.6 3.7 %collective-permute-start.9 = (f32[16,128]{1,0:T(8,128)S(1)}, f32[16,128]{1,0:T(8,128)S(1)}, u32[]{:S(2)}, u32[]{:S(2)}) collective-permute-start(f32[16,128]{1,0:T(8,128)S(1)} %add.9), channel_id=1, source_target_pairs={{0,2},{2,0},{1,3},{3,1},{4,6},{6,4},{5,7},{7,5},{8,10},{10,8},{9,1... | collective-permute-start | bytes 24584 | tf_op jit(solution)/shard_map/ppermute | solution.py:621
  37.4 3.7 %collective-permute-start.10 = (f32[16,128]{1,0:T(8,128)S(1)}, f32[16,128]{1,0:T(8,128)S(1)}, u32[]{:S(2)}, u32[]{:S(2)}) collective-permute-start(f32[16,128]{1,0:T(8,128)S(1)} %add.10), channel_id=1, source_target_pairs={{0,4},{4,0},{8,12},{12,8},{1,5},{5,1},{9,13},{13,9},{2,6},{6,2},{1... | collective-permute-start | bytes 24584 | tf_op jit(solution)/shard_map/ppermute | solution.py:689
  41.0 4.9 %copy-start.1 = (f32[48]{0:T(128)S(1)}, f32[48]{0:T(128)}, u32[]{:S(2)}) copy-start(f32[48]{0:T(128)} %coefficients.1) | copy-start | bytes 580
  41.0 4.9 %collective-permute-start.11 = (f32[16,128]{1,0:T(8,128)S(1)}, f32[16,128]{1,0:T(8,128)S(1)}, u32[]{:S(2)}, u32[]{:S(2)}) collective-permute-start(f32[16,128]{1,0:T(8,128)S(1)} %add.11.mine), channel_id=1, source_target_pairs={{0,8},{4,12},{8,0},{12,4},{1,9},{5,13},{9,1},{13,5},{2,10},{6,14},... | collective-permute-start | bytes 24584 | tf_op jit(solution)/shard_map/ppermute | solution.py:689
where the time goes:
time: 47.6 us; the launch traced here: 47.4 us
  starting transfers between devices  18.4 us (39%)
  Pallas kernels  14.7 us (31%)
  waiting for transfers between devices  12.6 us (26%)
  local copies, waits for them, and re-layouts  0.87 us (2%)
  between operations  0.73 us (2%)
    pallas_call x4, Pallas kernels, call(): pl.pallas_call(kernel, out_shape=outputs, in_specs=[VMEM_SPEC] * len(inpu...  11.9 us
    ppermute x2, starting transfers between devices, exchange(): lax.ppermute(jnp.where(even, first, last), 'down', far)  6.06 us
    ppermute x2, starting transfers between devices, body(): lax.ppermute(partial, 'down', [(i, i ^ distance) for i in range(down)])  5.29 us
    ppermute x2, waiting for transfers between devices, exchange(): lax.ppermute(jnp.concatenate([own, depth_halo], axis=0), 'cross', [(0, 1)...  4.4 us
    ppermute x2, starting transfers between devices, exchange(): lax.ppermute(jnp.concatenate([own, depth_halo], axis=0), 'cross', [(0, 1)...  4.38 us
    ppermute x2, waiting for transfers between devices, body(): lax.ppermute(partial, 'down', [(i, i ^ distance) for i in range(down)])  3.26 us
    ppermute x2, waiting for transfers between devices, shared(): lax.ppermute(value, axes, [(i, i ^ k) for i in range(peers)])  2.83 us
    ppermute x2, starting transfers between devices, shared(): lax.ppermute(value, axes, [(i, i ^ k) for i in range(peers)])  2.11 us
  transfers between devices with their start and end apart: 12, of which 9 were waited for; matrix products, arithmetic and copies ran while one was open for 2% of the time, Pallas kernels for 17%

commit v1 on v0

--- a/solution.py
+++ b/solution.py
@@ -115,7 +115,9 @@
                 return read(before if y == 0 else after, a * 2 + slot)
             return read(diag_before if y == 0 else diag_after, a)
         b = 1 if y == 0 else 0
-        return read(sides[0], a * 4 + b * 2 + slot if slot < 2 else 8 + a * 2 + b)
+        if slot < 2:
+            return read(sides[0], a * 4 + b * 2 + slot)
+        return read(sides[0], 8 + a * 2 + b) if len(sides) == 1 else read(sides[1], a * 2 + b)
 
     return cell
 
@@ -143,11 +145,12 @@
     return (x - 1.5, y - 1.5, (-1.0, 1.0, 3.0)[slot] * side)
 
 
-def extended_cells(xs, depth):
-    for k, x in enumerate(xs):
-        for y in range(4):
-            for slot in range(3):
-                yield x, y, slot, ((k * 4 + y) * 3 + slot) * 8, centre_of(x, y, slot, depth)
+BLOCK = tuple((x, y, slot) for x in (1, 2) for y in (1, 2) for slot in (0, 1))
+PLANE = tuple(
+    (x, y, slot) for x in (1, 2) for y in range(4) for slot in range(3) if (x, y, slot) not in BLOCK
+)
+INSIDE = tuple((x, y, slot) for x in (1, 2) for y in range(4) for slot in range(3))
+OUTSIDE = tuple((x, y, slot) for x in (0, 3) for y in range(4) for slot in range(3))
 
 
 def stepped_state(old, speed, centre):
@@ -156,42 +159,39 @@
     return (old[0:3] + TIME_STEP * speed[0:3]) + shift, speed[0:3], old[6:8]
 
 
-def contact_scratch(width):
+def contact_scratch(cells, width):
+    rows = len(cells)
     return [
-        pltpu.VMEM((24 * 8, S), F32),
+        pltpu.VMEM((rows * 8, S), F32),
         pltpu.VMEM((8 * 8, S), F32),
-        pltpu.VMEM((8 * 24, S), jnp.int32),
-        pltpu.VMEM((8 * 24, S), jnp.int32),
-        pltpu.VMEM((8 * 24, S), jnp.int32),
-        pltpu.VMEM((8 * 24, S), jnp.int32),
+        pltpu.VMEM((8 * rows, S), jnp.int32),
+        pltpu.VMEM((8 * rows, S), jnp.int32),
+        pltpu.VMEM((8 * rows, S), jnp.int32),
+        pltpu.VMEM((8 * rows, S), jnp.int32),
         pltpu.VMEM((18 * 8 * S, 32), F32),
         pltpu.VMEM((width * 8 * 8, S), F32),
     ]
 
 
-def contact_sums(xs, width, scratch):
+def contact_sums(cells, width, chunk, scratch):
     local_ref, mine_ref, index_ref, base_ref, amount_ref, chosen_ref, list_ref, sum_ref = scratch
-    together = xs[1] - xs[0] == 1
-    span = 24 if together else 16
+    count = len(cells)
+    span = 16 if cells == OUTSIDE else count
 
     def first_row(a):
-        return 0 if together or a == 0 else 8
+        return 8 if cells == OUTSIDE and a == 1 else 0
 
     def beside(a, b, z):
         return [
-            (k * 4 + y) * 3 + slot
-            for k, x in enumerate(xs)
-            if abs(x - 1 - a) <= 1
-            for y in range(b, b + 3)
-            for slot in range(3 if z == 1 else 2)
+            n
+            for n, (x, y, slot) in enumerate(cells)
+            if abs(x - 1 - a) <= 1 and abs(y - 1 - b) <= 1 and abs(slot - z) <= 1
         ]
 
     sum_ref[...] = jnp.zeros((width * 64, S), F32)
-    place = [local_ref[pl.ds(k, 24, stride=8), :] for k in range(3)]
-    radius = local_ref[pl.ds(6, 24, stride=8), :]
-    rows = row_ids((24, S))
-    row_x = jnp.where(rows < 12, xs[0], xs[1])
-    row_y, row_slot = (rows // 3) % 4, rows % 3
+    place = [local_ref[pl.ds(k, count, stride=8), :] for k in range(3)]
+    radius = local_ref[pl.ds(6, count, stride=8), :]
+    rows = row_ids((count, S))
     masks = []
     for c, (a, b, z) in enumerate(CELLS):
         mine = mine_ref[c * 8 : c * 8 + 8, :]
@@ -200,11 +200,11 @@
         high = jnp.max(jnp.where(live, mine, -1e9), axis=1, keepdims=True)
         part = slice(first_row(a), first_row(a) + span)
         reach = radius[part] + high[6:7]
-        near = jnp.logical_and(row_y[part] >= b, row_y[part] <= b + 2)
-        if not together:
-            near = jnp.logical_and(near, row_x[part] == xs[a])
-        if z == 0:
-            near = jnp.logical_and(near, row_slot[part] < 2)
+        near = reach > 0.0
+        inside = set(beside(a, b, z))
+        for n in range(part.start, part.stop):
+            if n not in inside:
+                near = jnp.logical_and(near, rows[part] != n)
         for k in range(3):
             near = jnp.logical_and(near, place[k][part] + reach > low[k : k + 1])
             near = jnp.logical_and(near, place[k][part] - reach < high[k : k + 1])
@@ -219,8 +219,8 @@
         part = amount[c * span : (c + 1) * span]
         base = matmul(before, part.astype(BF16))
         base_ref[c * span : (c + 1) * span, :] = base.astype(jnp.int32)
-        count = base[span - 1 : span] + part[span - 1 : span]
-        total = count if total is None else jnp.maximum(total, count)
+        listed = base[span - 1 : span] + part[span - 1 : span]
+        total = listed if total is None else jnp.maximum(total, listed)
     most = total.astype(jnp.int32)[0, 0]
     amount_ref[0 : 8 * span, :] = amount.astype(jnp.int32)
     wanted = lane_ids((8 * span, S)).astype(F32)
@@ -247,9 +247,9 @@
             rest = tile - high
             middle = rest.astype(BF16).astype(F32)
             turned = jnp.transpose(jnp.concatenate([high, middle, rest - middle, tile], axis=0))
-            for part in range(4):
-                start = pl.multiple_of(t * (8 * S) + (part * 8 + c) * 32, 32)
-                list_ref[pl.ds(start, 32), :] = turned[part * 32 : part * 32 + 32]
+            for part in range(S // chunk):
+                start = pl.multiple_of(t * (8 * S) + (part * 8 + c) * chunk, chunk)
+                list_ref[pl.ds(start, chunk), :] = turned[part * chunk : (part + 1) * chunk]
         return carry
 
     gather_tiles(0, 0)
@@ -261,14 +261,14 @@
     selector = one_hot(selector)
 
     def pair_step(step, carry):
-        every = list_ref[pl.ds(pl.multiple_of(step * 256, 256), 256), :]
+        every = list_ref[pl.ds(pl.multiple_of(step * (8 * chunk), 8 * chunk), 8 * chunk), :]
         spread = matmul(every.astype(BF16), selector)
         for c in range(8):
-            listed = every[c * 32 : c * 32 + 32]
+            listed = every[c * chunk : (c + 1) * chunk]
             me = [jnp.broadcast_to(mine_ref[c * 8 + k : c * 8 + k + 1, :], (8, S)) for k in range(7)]
             added = [None] * width
-            for block in range(4):
-                row = c * 32 + block * 8
+            for block in range(chunk // 8):
+                row = c * chunk + block * 8
                 other = [spread[row : row + 8, k * S : (k + 1) * S] for k in range(SPREAD)]
                 other += [
                     jnp.broadcast_to(listed[block * 8 : block * 8 + 8, 24 + k : 25 + k], (8, S))
@@ -292,7 +292,7 @@
                 sum_ref[row : row + 8, :] += added[k]
         return carry
 
-    lax.fori_loop(0, (most + 31) // 32, pair_step, 0)
+    lax.fori_loop(0, (most + (chunk - 1)) // chunk, pair_step, 0)
     out = []
     for k in range(width):
         parts = [sum_ref[pl.ds(k * 64 + sub, 8, stride=8), :] for sub in range(8)]
@@ -307,28 +307,43 @@
     return scaled * scaled * scaled
 
 
-def step_inside(*refs):
-    pieces, sums_out, scratch = refs[:-9], refs[-9], refs[-8:]
-    depth = lax.axis_index("depth")
-    cell = plane_reader(pieces, 8)
-    for x, y, slot, start, centre in extended_cells((1, 2), depth):
-        scratch[0][start : start + 8, :] = local_state(cell(x, y, slot), centre)
-    for c, (a, b, z) in enumerate(CELLS):
-        start = ((a * 4 + b + 1) * 3 + z) * 8
-        scratch[1][c * 8 : c * 8 + 8, :] = scratch[0][start : start + 8, :]
-    sums_out[...] = contact_sums((1, 2), 3, scratch)
-
-
-def step_outside(own, sums_in, near, far, own_out, inner_out, *scratch):
-    depth = lax.axis_index("depth")
-    cell = down_reader((near, far), 8)
-    for x, y, slot, start, centre in extended_cells((0, 3), depth):
-        scratch[0][start : start + 8, :] = local_state(cell(x, y, slot), centre)
+def fill_start(cells, read, own, depth, scratch):
+    for n, (x, y, slot) in enumerate(cells):
+        scratch[0][n * 8 : n * 8 + 8, :] = local_state(read(x, y, slot), centre_of(x, y, slot, depth))
     for c, (a, b, z) in enumerate(CELLS):
         scratch[1][c * 8 : c * 8 + 8, :] = local_state(
             own[c * 8 : c * 8 + 8, :], centre_of(a + 1, b + 1, z, depth)
         )
-    sums = sums_in[...] + contact_sums((0, 3), 3, scratch)
+
+
+def place_state(ref, start, state):
+    ref[start : start + 3, :] = state[0]
+    ref[start + 3 : start + 6, :] = state[1]
+    ref[start + 6 : start + 8, :] = state[2]
+
+
+def fill_stepped(cells, read, speed, own, own_speed, depth, scratch):
+    for n, (x, y, slot) in enumerate(cells):
+        state = stepped_state(read(x, y, slot), speed(x, y, slot), centre_of(x, y, slot, depth))
+        place_state(scratch[0], n * 8, state)
+    for c, (a, b, z) in enumerate(CELLS):
+        state = stepped_state(
+            own[c * 8 : c * 8 + 8, :],
+            own_speed[c * 4 : c * 4 + 4, :],
+            centre_of(a + 1, b + 1, z, depth),
+        )
+        place_state(scratch[1], c * 8, state)
+
+
+def step_inside(*refs):
+    pieces, sums_out, scratch = refs[:-9], refs[-9], refs[-8:]
+    fill_start(INSIDE, plane_reader(pieces, 8), pieces[0], lax.axis_index("depth"), scratch)
+    sums_out[...] = contact_sums(INSIDE, 3, 64, scratch)
+
+
+def step_outside(own, sums_in, near, far, own_out, inner_out, *scratch):
+    fill_start(OUTSIDE, down_reader((near, far), 8), own, lax.axis_index("depth"), scratch)
+    sums = sums_in[...] + contact_sums(OUTSIDE, 3, 32, scratch)
     radius = own[pl.ds(6, 8, stride=8), :]
     safe_mass = jnp.where(radius > 0.0, mass_of(radius), 1.0)
     for k in range(3):
@@ -341,23 +356,17 @@
         inner_out[column * 4 : column * 4 + 4, :] = own_out[column * 8 + 4 : column * 8 + 8, :]
 
 
-def place_state(ref, start, state):
-    ref[start : start + 3, :] = state[0]
-    ref[start + 3 : start + 6, :] = state[1]
-    ref[start + 6 : start + 8, :] = state[2]
-
-
-def field_inside(*refs):
-    count = (len(refs) - 9) // 2
-    pieces, speeds, sums_out, scratch = refs[:count], refs[count : 2 * count], refs[-9], refs[-8:]
-    depth = lax.axis_index("depth")
-    cell, speed = plane_reader(pieces, 8), plane_reader(speeds, 4)
-    for x, y, slot, start, centre in extended_cells((1, 2), depth):
-        place_state(scratch[0], start, stepped_state(cell(x, y, slot), speed(x, y, slot), centre))
-    for c, (a, b, z) in enumerate(CELLS):
-        start = ((a * 4 + b + 1) * 3 + z) * 8
-        scratch[1][c * 8 : c * 8 + 8, :] = scratch[0][start : start + 8, :]
-    sums_out[...] = contact_sums((1, 2), 9, scratch)
+def field_block(own, own_speed, sums_out, *scratch):
+    read, speed = plane_reader((own, None), 8), plane_reader((own_speed, None), 4)
+    fill_stepped(BLOCK, read, speed, own, own_speed, lax.axis_index("depth"), scratch)
+    sums_out[...] = contact_sums(BLOCK, 9, 64, scratch)
+
+
+def field_plane(split_at, sums_in, *refs):
+    pieces, speeds, sums_out, scratch = refs[:split_at], refs[split_at:-9], refs[-9], refs[-8:]
+    read, speed = plane_reader(pieces, 8), plane_reader(speeds, 4)
+    fill_stepped(PLANE, read, speed, pieces[0], speeds[0], lax.axis_index("depth"), scratch)
+    sums_out[...] = sums_in[...] + contact_sums(PLANE, 9, 32, scratch)
 
 
 def field_outside(
@@ -367,17 +376,9 @@
     down = lax.axis_index("down")
     cross = lax.axis_index("cross")
     mine_ref = scratch[1]
-    cell, speed = down_reader((near_old, far_old), 8), down_reader((near_speed, far_speed), 4)
-    for x, y, slot, start, centre in extended_cells((0, 3), depth):
-        place_state(scratch[0], start, stepped_state(cell(x, y, slot), speed(x, y, slot), centre))
-    for c, (a, b, z) in enumerate(CELLS):
-        state = stepped_state(
-            own[c * 8 : c * 8 + 8, :],
-            own_speed[c * 4 : c * 4 + 4, :],
-            centre_of(a + 1, b + 1, z, depth),
-        )
-        place_state(mine_ref, c * 8, state)
-    sums = sums_in[...] + contact_sums((0, 3), 9, scratch)
+    read, speed = down_reader((near_old, far_old), 8), down_reader((near_speed, far_speed), 4)
+    fill_stepped(OUTSIDE, read, speed, own, own_speed, depth, scratch)
+    sums = sums_in[...] + contact_sums(OUTSIDE, 9, 32, scratch)
     force_out[...] = sums[0:24]
     radius = own[pl.ds(6, 8, stride=8), :]
     mass = jnp.where(radius > 0.0, mass_of(radius), 0.0)
@@ -553,7 +554,7 @@
     return [(i, (i + step) % peers) for i in range(peers)]
 
 
-def exchange(own, inner, height):
+def exchange(own, inner, height, joined, beside=None):
     cross = lax.axis_size("cross")
 
     def cells(block, first, count):
@@ -561,17 +562,23 @@
 
     depth_halo = lax.ppermute(inner, "depth", [(0, 1), (1, 0)])
     if cross == 2:
-        side = lax.ppermute(
-            jnp.concatenate([own, depth_halo], axis=0), "cross", [(0, 1), (1, 0)]
-        )
-        sides = [side]
+        if joined:
+            side = lax.ppermute(
+                jnp.concatenate([own, depth_halo], axis=0), "cross", [(0, 1), (1, 0)]
+            )
+            diag = cells(side, 8, 4)
+            sides = [side]
+        else:
+            side = lax.ppermute(own, "cross", [(0, 1), (1, 0)])
+            diag = lax.ppermute(inner, ("cross", "depth"), [(i, 3 - i) for i in range(4)])
+            sides = [side, diag]
 
         def lateral(x):
             return [
                 cells(side, x * 4 + 2, 2),
                 cells(side, x * 4, 2),
-                cells(side, 8 + x * 2 + 1, 1),
-                cells(side, 8 + x * 2, 1),
+                cells(diag, x * 2 + 1, 1),
+                cells(diag, x * 2, 1),
             ]
 
     else:
@@ -600,6 +607,9 @@
 
     downs = lax.axis_size("down")
     last, first = face(1), face(0)
+    if beside is not None:
+        mine, depth_halo = lax.optimization_barrier((own, depth_halo))
+        last, first, result = lax.optimization_barrier((last, first, beside(mine)))
     if downs % 2 == 0:
         even = lax.rem(lax.axis_index("down"), 2) == 0
         near = [(i, i ^ 1) for i in range(downs)]
@@ -613,6 +623,8 @@
             lax.ppermute(last, "down", ring("down", 1)),
             lax.ppermute(first, "down", ring("down", -1)),
         ]
+    if beside is not None:
+        return [own, depth_halo] + sides, outside, result
     return [own, depth_halo] + sides, outside
 
 
@@ -665,25 +677,37 @@
         compiler_params=pltpu.CompilerParams(vmem_limit_bytes=60 * 1024 * 1024),
         name="pack",
     )(counts, positions, velocities, sphere_radii)
-    inside, outside = exchange(own, inner, 8)
-    sums = call(step_inside, inside, rows(24), contact_scratch(3), "step_inside", 1 << 31)
+    inside, outside = exchange(own, inner, 8, True)
+    sums = call(step_inside, inside, rows(24), contact_scratch(INSIDE, 3), "step_inside", 1 << 31)
     own_speed, inner_speed = call(
-        step_outside, [own, sums] + outside, (rows(32), rows(16)), contact_scratch(3), "step_outside", 1 << 30
-    )
-    inside_speed, outside_speed = exchange(own_speed, inner_speed, 4)
+        step_outside, [own, sums] + outside, (rows(32), rows(16)), contact_scratch(OUTSIDE, 3), "step_outside", 1 << 30
+    )
+    inside_speed, outside_speed, sums = exchange(
+        own_speed,
+        inner_speed,
+        4,
+        False,
+        lambda speed: call(
+            field_block, [own, speed], rows(72), contact_scratch(BLOCK, 9), "field_block", 1 << 31
+        ),
+    )
     sums = call(
-        field_inside, inside + inside_speed, rows(72), contact_scratch(9), "field_inside", 1 << 31
+        functools.partial(field_plane, len(inside)),
+        [sums] + inside + inside_speed,
+        rows(72),
+        contact_scratch(PLANE, 9),
+        "field_plane",
+        1 << 31,
     )
     force, partial = call(
         functools.partial(field_outside, grid),
         [own, own_speed, sums] + outside + outside_speed,
         (rows(24), jax.ShapeDtypeStruct((16, nodes), F32)),
-        [pltpu.VMEM((16, 8 * S), F32)] + contact_scratch(9),
+        [pltpu.VMEM((16, 8 * S), F32)] + contact_scratch(OUTSIDE, 9),
         "field_outside",
         1 << 30,
     )
-    for axis in ("depth", "cross"):
-        partial = tree_sum(shared(partial, axis, lax.axis_size(axis)))
+    partial = tree_sum(shared(partial, ("cross", "depth"), cross * depth))
     distance = 1
     while distance < down:
         other = lax.ppermute(partial, "down", [(i, i ^ distance) for i in range(down)])

time: 47.6 us -> 47.9 us (level)
  starting transfers between devices: 18.4 us -> 13.9 us
  waiting for transfers between devices: 12.6 us -> 16 us
  Pallas kernels: 14.7 us -> 15.9 us
    ppermute x2, starting transfers between devices: 5.29 us -> 0.86 us  [body(): lax.ppermute(partial, 'down', [(i, i ^ distance) for i in range(down)])]
    ppermute x2, waiting for transfers between devices: 3.26 us -> 7.42 us  [body(): lax.ppermute(partial, 'down', [(i, i ^ distance) for i in range(down)])]
    ppermute x2, waiting for transfers between devices: 0.01 us -> 2.76 us  [exchange(): lax.ppermute(jnp.where(even, first, last), 'down', far)]
    ppermute x2 -> x1, waiting for transfers between devices: 4.4 us -> 2.07 us  [exchange(): lax.ppermute(jnp.concatenate([own, depth_halo], axis=0), 'cross', [(0, 1)...]
    ppermute x2, starting transfers between devices: 0.59 us -> 2.11 us  [exchange(): depth_halo = lax.ppermute(inner, 'depth', [(0, 1), (1, 0)])]
    ppermute x2 -> x1, starting transfers between devices: 4.38 us -> 2.89 us  [exchange(): lax.ppermute(jnp.concatenate([own, depth_halo], axis=0), 'cross', [(0, 1)...]
    pallas_call x4 -> x5, Pallas kernels: 11.9 us -> 13 us  [call(): pl.pallas_call(kernel, out_shape=outputs, in_specs=[VMEM_SPEC] * len(inpu...]
    ppermute x2 -> x3, waiting for transfers between devices: 2.83 us -> 1.83 us  [shared(): lax.ppermute(value, axes, [(i, i ^ k) for i in range(peers)])]
  transfers between devices with their start and end apart: 12 -> 14, of which waited for: 9 -> 10; matrix products, arithmetic and copies ran while one was open for 2% -> 2% of each run, Pallas kernels for 17% -> 19%
where the time goes in v1:
time: 47.9 us; the launch traced here: 47.5 us
  waiting for transfers between devices  16 us (33%)
  Pallas kernels  15.9 us (33%)
  starting transfers between devices  13.9 us (29%)
  local copies, waits for them, and re-layouts  0.87 us (2%)
  between operations  0.74 us (2%)
    pallas_call x5, Pallas kernels, call(): pl.pallas_call(kernel, out_shape=outputs, in_specs=[VMEM_SPEC] * len(inpu...  13 us
    ppermute x2, waiting for transfers between devices, body(): lax.ppermute(partial, 'down', [(i, i ^ distance) for i in range(down)])  7.42 us
    ppermute x2, starting transfers between devices, exchange(): lax.ppermute(jnp.where(even, first, last), 'down', far)  5.51 us
    ppermute x1, starting transfers between devices, exchange(): lax.ppermute(jnp.concatenate([own, depth_halo], axis=0), 'cross', [(0, 1)...  2.89 us
    ppermute x2, waiting for transfers between devices, exchange(): lax.ppermute(jnp.where(even, first, last), 'down', far)  2.76 us
    ppermute x2, starting transfers between devices, exchange(): depth_halo = lax.ppermute(inner, 'depth', [(0, 1), (1, 0)])  2.11 us
    ppermute x1, waiting for transfers between devices, exchange(): lax.ppermute(jnp.concatenate([own, depth_halo], axis=0), 'cross', [(0, 1)...  2.07 us
    ppermute x3, starting transfers between devices, shared(): lax.ppermute(value, axes, [(i, i ^ k) for i in range(peers)])  1.89 us
  transfers between devices with their start and end apart: 14, of which 10 were waited for; matrix products, arithmetic and copies ran while one was open for 2% of the time, Pallas kernels for 19%

profile of v1, /device:TPU:0, one launch (start us, length us, event | category | flops | bytes accessed | tf_op | source)
XLA Modules:
  0.0 47.5 jit_solution(3198443938054658962)
XLA Ops:
  0.6 1.4 %pack.1 = (f32[64,128]{1,0:T(8,128)}, f32[32,128]{1,0:T(8,128)}) custom-call(s32[2,2,2]{2,1,0:T(2,128)} %counts_hbm.1, f32[3,2,2,2,128]{4,3,2,1,0:T(2,128)} %positions_hbm.1, f32[3,2,2,2,128]{4,3,2,1,0:T(2,128)} %velocities_hbm.1, f32[2,2,2,128]{3,2,1,0:T(2,128)} %radii_hbm.1), custom_call_target="tpu_custom_call" | custom-call | tf_op jit(solution)/shard_map/pack/pallas_call | solution.py:665
  2.0 0.5 %collective-permute-start = (f32[32,128]{1,0:T(8,128)}, f32[32,128]{1,0:T(8,128)S(1)}, u32[]{:S(2)}, u32[]{:S(2)}) collective-permute-start(f32[32,128]{1,0:T(8,128)} %get-tuple-element.22), channel_id=1, source_target_pairs={{0,1},{1,0},{2,3},{3,2},{4,5},{5,4},{6,7},{7,6},{8,9},{9,8},{10,11... | collective-permute-start | bytes 49160 | tf_op jit(solution)/shard_map/ppermute | solution.py:563
  2.6 0.8 %constant_dynamic-update-slice_fusion.11 = (f32[96,128]{1,0:T(8,128)S(1)}, f32[96,128]{1,0:T(8,128)S(1)}) fusion(f32[64,128]{1,0:T(8,128)} %get-tuple-element.21.refs_0_.own), kind=kLoop, calls=%fused_computation.12 | loop fusion | bytes 65536
  3.4 0.3 collective-permute-done.refs_1_
  3.6 2.9 %collective-permute-start.1 = (f32[96,128]{1,0:T(8,128)S(1)}, f32[96,128]{1,0:T(8,128)S(1)}, u32[]{:S(2)}, u32[]{:S(2)}) collective-permute-start(f32[96,128]{1,0:T(8,128)S(1)} %pad_maximum_fusion), channel_id=1, source_target_pairs={{0,2},{2,0},{1,3},{3,1},{4,6},{6,4},{5,7},{7,5},{8,10},{10,8},{9,1... | collective-permute-start | bytes 147464 | tf_op jit(solution)/shard_map/ppermute | solution.py:566
  6.5 2.1 %collective-permute-done.1.refs_2_ = f32[96,128]{1,0:T(8,128)S(1)} collective-permute-done((f32[96,128]{1,0:T(8,128)S(1)}, f32[96,128]{1,0:T(8,128)S(1)}, u32[]{:S(2)}, u32[]{:S(2)}) %collective-permute-start.1) | collective-permute-done | bytes 49184 | tf_op jit(solution)/shard_map/ppermute | solution.py:566
  8.6 4.2 %collective-permute-start.3 = (f32[96,128]{1,0:T(8,128)S(1)}, f32[96,128]{1,0:T(8,128)S(1)}, u32[]{:S(2)}, u32[]{:S(2)}) collective-permute-start(f32[96,128]{1,0:T(8,128)S(1)} %get-tuple-element.37), channel_id=1, source_target_pairs={{0,12},{4,8},{8,4},{12,0},{1,13},{5,9},{9,5},{13,1},{2,14},{6,10},... | collective-permute-start | bytes 147464 | tf_op jit(solution)/shard_map/ppermute | solution.py:619
  12.8 3.3 %step_inside.1.sums_in = f32[24,128]{1,0:T(8,128)S(1)} custom-call(f32[64,128]{1,0:T(8,128)S(1)} %copy-done, f32[32,128]{1,0:T(8,128)S(1)} %collective-permute-done.refs_1_, f32[96,128]{1,0:T(8,128)S(1)} %collective-permute-done.1.refs_2_), custom_call_target="tpu_custom_call" | custom-call | flops 2147483648 | bytes 1048576 | tf_op jit(solution)/shard_map/step_inside/pallas_call | solution.py:654
  16.2 0.0 collective-permute-done.3.far.far_old
  16.2 0.7 %collective-permute-done.2.near.near_old = f32[96,128]{1,0:T(8,128)S(1)} collective-permute-done((f32[96,128]{1,0:T(8,128)S(1)}, f32[96,128]{1,0:T(8,128)S(1)}, u32[]{:S(2)}, u32[]{:S(2)}) %collective-permute-start.2) | collective-permute-done | bytes 49184 | tf_op jit(solution)/shard_map/ppermute | solution.py:618
  16.9 1.6 %step_outside.1 = (f32[32,128]{1,0:T(8,128)S(1)}, f32[16,128]{1,0:T(8,128)S(1)}) custom-call(f32[64,128]{1,0:T(8,128)S(1)} %copy-done, f32[24,128]{1,0:T(8,128)S(1)} %step_inside.1.sums_in, f32[96,128]{1,0:T(8,128)S(1)} %collective-permute-done.2.near.near_old, f32[96,128]{1,0:T(8,128)S(1)} %collective-permute-done.3.far.far_old), custom_call_target="tpu_custom_call" | custom-call | flops 1073741824 | bytes 1048576 | tf_op jit(solution)/shard_map/step_outside/pallas_call | solution.py:654
  18.5 0.1 collective-permute-start.6
  18.5 1.6 %collective-permute-start.4 = (f32[16,128]{1,0:T(8,128)S(1)}, f32[16,128]{1,0:T(8,128)S(1)}, u32[]{:S(2)}, u32[]{:S(2)}) collective-permute-start(f32[16,128]{1,0:T(8,128)S(1)} %get-tuple-element.24), channel_id=1, source_target_pairs={{0,1},{1,0},{2,3},{3,2},{4,5},{5,4},{6,7},{7,6},{8,9},{9,8},{10,11... | collective-permute-start | bytes 24584 | tf_op jit(solution)/shard_map/ppermute | solution.py:563
  20.1 0.5 %collective-permute-start.5 = (f32[32,128]{1,0:T(8,128)S(1)}, f32[32,128]{1,0:T(8,128)S(1)}, u32[]{:S(2)}, u32[]{:S(2)}) collective-permute-start(f32[32,128]{1,0:T(8,128)S(1)} %get-tuple-element.25.own_speed.refs_3_.speed), channel_id=1, source_target_pairs={{0,2},{2,0},{1,3},{3,1},{4,6},{6,4},{5,7},{7,5},{8,10},{10,8},{9,1... | collective-permute-start | bytes 49160 | tf_op jit(solution)/shard_map/ppermute | solution.py:572
  20.7 0.3 collective-permute-done.4.refs_4_
  21.0 0.7 %collective-permute-done.6.refs_6_ = f32[16,128]{1,0:T(8,128)S(1)} collective-permute-done((f32[16,128]{1,0:T(8,128)S(1)}, f32[16,128]{1,0:T(8,128)S(1)}, u32[]{:S(2)}, u32[]{:S(2)}) %collective-permute-start.6) | collective-permute-done | bytes 8224 | tf_op jit(solution)/shard_map/ppermute | solution.py:573
  21.6 4.1 %field_block.1.sums_in = f32[72,128]{1,0:T(8,128)S(1)} custom-call(f32[64,128]{1,0:T(8,128)S(1)} %copy-done, f32[32,128]{1,0:T(8,128)S(1)} %get-tuple-element.25.own_speed.refs_3_.speed), custom_call_target="tpu_custom_call" | custom-call | flops 2147483648 | bytes 1048576 | tf_op jit(solution)/shard_map/field_block/pallas_call | solution.py:654
  25.8 1.3 %collective-permute-start.8 = (f32[48,128]{1,0:T(8,128)S(1)}, f32[48,128]{1,0:T(8,128)S(1)}, u32[]{:S(2)}, u32[]{:S(2)}) collective-permute-start(f32[48,128]{1,0:T(8,128)S(1)} %get-tuple-element.39), channel_id=1, source_target_pairs={{0,12},{4,8},{8,4},{12,0},{1,13},{5,9},{9,5},{13,1},{2,14},{6,10},... | collective-permute-start | bytes 73736 | tf_op jit(solution)/shard_map/ppermute | solution.py:619
  27.1 0.0 collective-permute-start.7
  27.1 1.6 %field_plane.1.sums_in = f32[72,128]{1,0:T(8,128)S(1)} custom-call(f32[72,128]{1,0:T(8,128)S(1)} %field_block.1.sums_in, f32[64,128]{1,0:T(8,128)S(1)} %copy-done, f32[32,128]{1,0:T(8,128)S(1)} %collective-permute-done.refs_1_, f32[96,128]{1,0:T(8,128)S(1)} %collective-permute-done.1.refs_2_, f32[32,128]{1,0:T(8,128)S(1)} %get-tuple-element.25.own_speed.refs_3_.speed, ...), custom_call_target="tpu_custom_call" | custom-call | flops 2147483648 | bytes 1048576 | tf_op jit(solution)/shard_map/field_plane/pallas_call | solution.py:654
  28.7 2.8 %collective-permute-done.8.far_speed = f32[48,128]{1,0:T(8,128)S(1)} collective-permute-done((f32[48,128]{1,0:T(8,128)S(1)}, f32[48,128]{1,0:T(8,128)S(1)}, u32[]{:S(2)}, u32[]{:S(2)}) %collective-permute-start.8) | collective-permute-done | bytes 24608 | tf_op jit(solution)/shard_map/ppermute | solution.py:619
  31.5 2.5 %field_outside.1 = (f32[24,128]{1,0:T(8,128)S(1)}, f32[16,128]{1,0:T(8,128)S(1)}) custom-call(f32[64,128]{1,0:T(8,128)S(1)} %copy-done, f32[32,128]{1,0:T(8,128)S(1)} %get-tuple-element.25.own_speed.refs_3_.speed, f32[72,128]{1,0:T(8,128)S(1)} %field_plane.1.sums_in, f32[96,128]{1,0:T(8,128)S(1)} %collective-permute-done.2.near.near_old, ...), custom_call_target="tpu_custom_call" | custom-call | flops 1073741824 | bytes 1048576 | tf_op jit(solution)/shard_map/field_outside/pallas_call | solution.py:654
  33.9 0.0 collective-permute-start.11
  33.9 1.5 %collective-permute-start.10 = (f32[16,128]{1,0:T(8,128)S(1)}, f32[16,128]{1,0:T(8,128)S(1)}, u32[]{:S(2)}, u32[]{:S(2)}) collective-permute-start(f32[16,128]{1,0:T(8,128)S(1)} %get-tuple-element.30), channel_id=1, source_target_pairs={{0,2},{1,3},{2,0},{3,1},{4,6},{5,7},{6,4},{7,5},{8,10},{9,11},{10,... | collective-permute-start | bytes 24584 | tf_op jit(solution)/shard_map/ppermute | solution.py:633
  35.5 0.4 collective-permute-start.9
  35.8 1.3 %collective-permute-done.11 = f32[16,128]{1,0:T(8,128)S(1)} collective-permute-done((f32[16,128]{1,0:T(8,128)S(1)}, f32[16,128]{1,0:T(8,128)S(1)}, u32[]{:S(2)}, u32[]{:S(2)}) %collective-permute-start.11) | collective-permute-done | bytes 8224 | tf_op jit(solution)/shard_map/ppermute | solution.py:633
  37.1 0.5 %collective-permute-done.10 = f32[16,128]{1,0:T(8,128)S(1)} collective-permute-done((f32[16,128]{1,0:T(8,128)S(1)}, f32[16,128]{1,0:T(8,128)S(1)}, u32[]{:S(2)}, u32[]{:S(2)}) %collective-permute-start.10) | collective-permute-done | bytes 8224 | tf_op jit(solution)/shard_map/ppermute | solution.py:633
  37.7 0.1 collective-permute-start.12
  37.8 3.7 %collective-permute-done.12 = f32[16,128]{1,0:T(8,128)S(1)} collective-permute-done((f32[16,128]{1,0:T(8,128)S(1)}, f32[16,128]{1,0:T(8,128)S(1)}, u32[]{:S(2)}, u32[]{:S(2)}) %collective-permute-start.12) | collective-permute-done | bytes 8224 | tf_op jit(solution)/shard_map/ppermute | solution.py:713
  41.4 0.8 %collective-permute-start.13 = (f32[16,128]{1,0:T(8,128)S(1)}, f32[16,128]{1,0:T(8,128)S(1)}, u32[]{:S(2)}, u32[]{:S(2)}) collective-permute-start(f32[16,128]{1,0:T(8,128)S(1)} %add.15.mine), channel_id=1, source_target_pairs={{0,8},{4,12},{8,0},{12,4},{1,9},{5,13},{9,1},{13,5},{2,10},{6,14},... | collective-permute-start | bytes 24584 | tf_op jit(solution)/shard_map/ppermute | solution.py:713
  42.2 3.8 %collective-permute-done.13.other = f32[16,128]{1,0:T(8,128)S(1)} collective-permute-done((f32[16,128]{1,0:T(8,128)S(1)}, f32[16,128]{1,0:T(8,128)S(1)}, u32[]{:S(2)}, u32[]{:S(2)}) %collective-permute-start.13) | collective-permute-done | bytes 8224 | tf_op jit(solution)/shard_map/ppermute | solution.py:713
  46.0 1.5 %library.1 = (f32[3,2,2,2,128]{4,3,2,1,0:T(2,128)}, f32[3,2,2,2,128]{4,3,2,1,0:T(2,128)}, f32[2,2,2]{2,1,0:T(2,128)}, f32[48,48]{1,0:T(8,128)}, f32[1,48]{1,0:T(1,128)}) custom-call(f32[48]{0:T(128)S(1)} %copy-done.1, f32[16,128]{1,0:T(8,128)S(1)} %add.15.mine, f32[16,128]{1,0:T(8,128)S(1)} %collective-permute-done.13.other, ...), custom_call_target="tpu_custom_call" | custom-call | tf_op jit(solution)/shard_map/library/pallas_call | solution.py:717
  (24 shorter events, 0.1 us)
Async XLA Ops:
  2.0 1.6 %collective-permute-start = (f32[32,128]{1,0:T(8,128)}, f32[32,128]{1,0:T(8,128)S(1)}, u32[]{:S(2)}, u32[]{:S(2)}) collective-permute-start(f32[32,128]{1,0:T(8,128)} %get-tuple-element.22), channel_id=1, source_target_pairs={{0,1},{1,0},{2,3},{3,2},{4,5},{5,4},{6,7},{7,6},{8,9},{9,8},{10,11... | collective-permute-start | bytes 49160 | tf_op jit(solution)/shard_map/ppermute | solution.py:563
  2.6 1.1 %copy-start = (f32[64,128]{1,0:T(8,128)S(1)}, f32[64,128]{1,0:T(8,128)}, u32[]{:S(2)}) copy-start(f32[64,128]{1,0:T(8,128)} %get-tuple-element.21.refs_0_.own) | copy-start | bytes 98308
  3.6 5.0 %collective-permute-start.1 = (f32[96,128]{1,0:T(8,128)S(1)}, f32[96,128]{1,0:T(8,128)S(1)}, u32[]{:S(2)}, u32[]{:S(2)}) collective-permute-start(f32[96,128]{1,0:T(8,128)S(1)} %pad_maximum_fusion), channel_id=1, source_target_pairs={{0,2},{2,0},{1,3},{3,1},{4,6},{6,4},{5,7},{7,5},{8,10},{10,8},{9,1... | collective-permute-start | bytes 147464 | tf_op jit(solution)/shard_map/ppermute | solution.py:566
  8.6 7.5 %collective-permute-start.3 = (f32[96,128]{1,0:T(8,128)S(1)}, f32[96,128]{1,0:T(8,128)S(1)}, u32[]{:S(2)}, u32[]{:S(2)}) collective-permute-start(f32[96,128]{1,0:T(8,128)S(1)} %get-tuple-element.37), channel_id=1, source_target_pairs={{0,12},{4,8},{8,4},{12,0},{1,13},{5,9},{9,5},{13,1},{2,14},{6,10},... | collective-permute-start | bytes 147464 | tf_op jit(solution)/shard_map/ppermute | solution.py:619
  12.8 4.1 %collective-permute-start.2 = (f32[96,128]{1,0:T(8,128)S(1)}, f32[96,128]{1,0:T(8,128)S(1)}, u32[]{:S(2)}, u32[]{:S(2)}) collective-permute-start(f32[96,128]{1,0:T(8,128)S(1)} %get-tuple-element.38), channel_id=1, source_target_pairs={{0,4},{4,0},{8,12},{12,8},{1,5},{5,1},{9,13},{13,9},{2,6},{6,2},{1... | collective-permute-start | bytes 147464 | tf_op jit(solution)/shard_map/ppermute | solution.py:618
  18.5 3.2 %collective-permute-start.6 = (f32[16,128]{1,0:T(8,128)S(1)}, f32[16,128]{1,0:T(8,128)S(1)}, u32[]{:S(2)}, u32[]{:S(2)}) collective-permute-start(f32[16,128]{1,0:T(8,128)S(1)} %get-tuple-element.24), channel_id=1, source_target_pairs={{0,3},{1,2},{2,1},{3,0},{4,7},{5,6},{6,5},{7,4},{8,11},{9,10},{10,... | collective-permute-start | bytes 24584 | tf_op jit(solution)/shard_map/ppermute | solution.py:573
  18.5 2.4 %collective-permute-start.4 = (f32[16,128]{1,0:T(8,128)S(1)}, f32[16,128]{1,0:T(8,128)S(1)}, u32[]{:S(2)}, u32[]{:S(2)}) collective-permute-start(f32[16,128]{1,0:T(8,128)S(1)} %get-tuple-element.24), channel_id=1, source_target_pairs={{0,1},{1,0},{2,3},{3,2},{4,5},{5,4},{6,7},{7,6},{8,9},{9,8},{10,11... | collective-permute-start | bytes 24584 | tf_op jit(solution)/shard_map/ppermute | solution.py:563
  20.1 5.6 %collective-permute-start.5 = (f32[32,128]{1,0:T(8,128)S(1)}, f32[32,128]{1,0:T(8,128)S(1)}, u32[]{:S(2)}, u32[]{:S(2)}) collective-permute-start(f32[32,128]{1,0:T(8,128)S(1)} %get-tuple-element.25.own_speed.refs_3_.speed), channel_id=1, source_target_pairs={{0,2},{2,0},{1,3},{3,1},{4,6},{6,4},{5,7},{7,5},{8,10},{10,8},{9,1... | collective-permute-start | bytes 49160 | tf_op jit(solution)/shard_map/ppermute | solution.py:572
  25.8 5.7 %collective-permute-start.8 = (f32[48,128]{1,0:T(8,128)S(1)}, f32[48,128]{1,0:T(8,128)S(1)}, u32[]{:S(2)}, u32[]{:S(2)}) collective-permute-start(f32[48,128]{1,0:T(8,128)S(1)} %get-tuple-element.39), channel_id=1, source_target_pairs={{0,12},{4,8},{8,4},{12,0},{1,13},{5,9},{9,5},{13,1},{2,14},{6,10},... | collective-permute-start | bytes 73736 | tf_op jit(solution)/shard_map/ppermute | solution.py:619
  27.1 4.4 %collective-permute-start.7 = (f32[48,128]{1,0:T(8,128)S(1)}, f32[48,128]{1,0:T(8,128)S(1)}, u32[]{:S(2)}, u32[]{:S(2)}) collective-permute-start(f32[48,128]{1,0:T(8,128)S(1)} %get-tuple-element.40), channel_id=1, source_target_pairs={{0,4},{4,0},{8,12},{12,8},{1,5},{5,1},{9,13},{13,9},{2,6},{6,2},{1... | collective-permute-start | bytes 73736 | tf_op jit(solution)/shard_map/ppermute | solution.py:618
  33.9 3.2 %collective-permute-start.11 = (f32[16,128]{1,0:T(8,128)S(1)}, f32[16,128]{1,0:T(8,128)S(1)}, u32[]{:S(2)}, u32[]{:S(2)}) collective-permute-start(f32[16,128]{1,0:T(8,128)S(1)} %get-tuple-element.30), channel_id=1, source_target_pairs={{0,3},{1,2},{2,1},{3,0},{4,7},{5,6},{6,5},{7,4},{8,11},{9,10},{10,... | collective-permute-start | bytes 24584 | tf_op jit(solution)/shard_map/ppermute | solution.py:633
  33.9 3.7 %collective-permute-start.10 = (f32[16,128]{1,0:T(8,128)S(1)}, f32[16,128]{1,0:T(8,128)S(1)}, u32[]{:S(2)}, u32[]{:S(2)}) collective-permute-start(f32[16,128]{1,0:T(8,128)S(1)} %get-tuple-element.30), channel_id=1, source_target_pairs={{0,2},{1,3},{2,0},{3,1},{4,6},{5,7},{6,4},{7,5},{8,10},{9,11},{10,... | collective-permute-start | bytes 24584 | tf_op jit(solution)/shard_map/ppermute | solution.py:633
  35.5 2.2 %collective-permute-start.9 = (f32[16,128]{1,0:T(8,128)S(1)}, f32[16,128]{1,0:T(8,128)S(1)}, u32[]{:S(2)}, u32[]{:S(2)}) collective-permute-start(f32[16,128]{1,0:T(8,128)S(1)} %get-tuple-element.30), channel_id=1, source_target_pairs={{0,1},{1,0},{2,3},{3,2},{4,5},{5,4},{6,7},{7,6},{8,9},{9,8},{10,11... | collective-permute-start | bytes 24584 | tf_op jit(solution)/shard_map/ppermute | solution.py:633
  37.7 3.7 %collective-permute-start.12 = (f32[16,128]{1,0:T(8,128)S(1)}, f32[16,128]{1,0:T(8,128)S(1)}, u32[]{:S(2)}, u32[]{:S(2)}) collective-permute-start(f32[16,128]{1,0:T(8,128)S(1)} %add_add_fusion), channel_id=1, source_target_pairs={{0,4},{4,0},{8,12},{12,8},{1,5},{5,1},{9,13},{13,9},{2,6},{6,2},{1... | collective-permute-start | bytes 24584 | tf_op jit(solution)/shard_map/ppermute | solution.py:713
  41.4 4.6 %copy-start.1 = (f32[48]{0:T(128)S(1)}, f32[48]{0:T(128)}, u32[]{:S(2)}) copy-start(f32[48]{0:T(128)} %coefficients.1) | copy-start | bytes 580
  41.4 4.5 %collective-permute-start.13 = (f32[16,128]{1,0:T(8,128)S(1)}, f32[16,128]{1,0:T(8,128)S(1)}, u32[]{:S(2)}, u32[]{:S(2)}) collective-permute-start(f32[16,128]{1,0:T(8,128)S(1)} %add.15.mine), channel_id=1, source_target_pairs={{0,8},{4,12},{8,0},{12,4},{1,9},{5,13},{9,1},{13,5},{2,10},{6,14},... | collective-permute-start | bytes 24584 | tf_op jit(solution)/shard_map/ppermute | solution.py:713

commit v2 on v1

--- a/solution.py
+++ b/solution.py
@@ -356,26 +356,59 @@
         inner_out[column * 4 : column * 4 + 4, :] = own_out[column * 8 + 4 : column * 8 + 8, :]
 
 
-def field_block(own, own_speed, sums_out, *scratch):
-    read, speed = plane_reader((own, None), 8), plane_reader((own_speed, None), 4)
-    fill_stepped(BLOCK, read, speed, own, own_speed, lax.axis_index("depth"), scratch)
-    sums_out[...] = contact_sums(BLOCK, 9, 64, scratch)
-
-
-def field_plane(split_at, sums_in, *refs):
-    pieces, speeds, sums_out, scratch = refs[:split_at], refs[split_at:-9], refs[-9], refs[-8:]
-    read, speed = plane_reader(pieces, 8), plane_reader(speeds, 4)
-    fill_stepped(PLANE, read, speed, pieces[0], speeds[0], lax.axis_index("depth"), scratch)
-    sums_out[...] = sums_in[...] + contact_sums(PLANE, 9, 32, scratch)
-
-
-def field_outside(
-    grid, own, own_speed, sums_in, near_old, far_old, near_speed, far_speed, force_out, node_out, moment_ref, *scratch
-):
+def field_weights(grid, own, own_speed, coefficients, high_out, low_out, chosen_out, model_out):
+    model_out[...] = coefficients[...]
     depth = lax.axis_index("depth")
     down = lax.axis_index("down")
     cross = lax.axis_index("cross")
-    mine_ref = scratch[1]
+    rows = row_ids((64, S))
+    near_x, near_y, near_z = rows // 16 - 1, (rows // 4) % 4 - 1, rows % 4 - 1
+    centres = [index.astype(F32) - 0.5 for index in (near_x, near_y, near_z)]
+    kernels = []
+    for c, (a, b, z) in enumerate(CELLS):
+        place = stepped_state(
+            own[c * 8 : c * 8 + 8, :],
+            own_speed[c * 4 : c * 4 + 4, :],
+            centre_of(a + 1, b + 1, z, depth),
+        )[0]
+        squared = jnp.zeros((64, S), F32)
+        for k in range(3):
+            gap = place[k : k + 1] - centres[k]
+            squared = squared + gap * gap
+        kernel = jnp.exp(squared * (-0.5 / (KERNEL_WIDTH * KERNEL_WIDTH))) / KERNEL_NORM
+        beside = jnp.logical_and(
+            jnp.logical_and(jnp.abs(near_x - a) <= 1, jnp.abs(near_y - b) <= 1),
+            jnp.abs(near_z - jnp.where(depth == z, 0, 1)) <= 1,
+        )
+        kernels.append(jnp.where(beside, kernel, 0.0))
+    kernel_high, kernel_low = split(jnp.concatenate(kernels, axis=1))
+    high_out[...] = kernel_high
+    low_out[...] = kernel_low.astype(BF16)
+    size_x, size_y, size_z = grid
+    nodes = size_x * size_y * size_z
+    lanes = lane_ids((64, nodes))
+    row = row_ids((64, nodes))
+    target_x = (down * 2 + row // 16 - 1 + size_x) % size_x
+    target_y = (cross * 2 + (row // 4) % 4 - 1 + size_y) % size_y
+    target_z = depth * 2 + row % 4 - 1
+    inside = jnp.logical_and(target_z >= 0, target_z < size_z)
+    target = (target_x * size_y + target_y) * size_z + target_z
+    chosen_out[...] = one_hot(jnp.logical_and(inside, lanes == target))
+
+
+def field_inside(*refs):
+    split_at = (len(refs) - 9) // 2
+    pieces, speeds, sums_out, scratch = refs[:split_at], refs[split_at:-9], refs[-9], refs[-8:]
+    read, speed = plane_reader(pieces, 8), plane_reader(speeds, 4)
+    fill_stepped(INSIDE, read, speed, pieces[0], speeds[0], lax.axis_index("depth"), scratch)
+    sums_out[...] = contact_sums(INSIDE, 9, 64, scratch)
+
+
+def field_outside(
+    own, own_speed, sums_in, near_old, far_old, near_speed, far_speed, kernel_high, kernel_low, chosen,
+    force_out, node_out, moment_ref, *scratch
+):
+    depth = lax.axis_index("depth")
     read, speed = down_reader((near_old, far_old), 8), down_reader((near_speed, far_speed), 4)
     fill_stepped(OUTSIDE, read, speed, own, own_speed, depth, scratch)
     sums = sums_in[...] + contact_sums(OUTSIDE, 9, 32, scratch)
@@ -388,41 +421,15 @@
     for m, moment in enumerate(moments):
         for c in range(8):
             moment_ref[m : m + 1, c * S : (c + 1) * S] = moment[c : c + 1]
-    rows = row_ids((64, S))
-    near_x, near_y, near_z = rows // 16 - 1, (rows // 4) % 4 - 1, rows % 4 - 1
-    centres = [index.astype(F32) - 0.5 for index in (near_x, near_y, near_z)]
-    kernels = []
-    for c, (a, b, z) in enumerate(CELLS):
-        squared = jnp.zeros((64, S), F32)
-        for k in range(3):
-            gap = mine_ref[c * 8 + k : c * 8 + k + 1, :] - centres[k]
-            squared = squared + gap * gap
-        kernel = jnp.exp(squared * (-0.5 / (KERNEL_WIDTH * KERNEL_WIDTH))) / KERNEL_NORM
-        beside = jnp.logical_and(
-            jnp.logical_and(jnp.abs(near_x - a) <= 1, jnp.abs(near_y - b) <= 1),
-            jnp.abs(near_z - jnp.where(depth == z, 0, 1)) <= 1,
-        )
-        kernels.append(jnp.where(beside, kernel, 0.0))
-    kernel_high, kernel_low = split(jnp.concatenate(kernels, axis=1))
     moment_high, moment_low = split(moment_ref[...])
     wide_part = matmul_turned(
-        jnp.concatenate([moment_high, moment_low.astype(BF16)], axis=0), kernel_high
-    )
-    near = wide_part[0:16] + wide_part[16:32] + matmul_turned(moment_high, kernel_low.astype(BF16))
-    size_x, size_y, size_z = grid
-    nodes = size_x * size_y * size_z
-    lanes = lane_ids((64, nodes))
-    row = row_ids((64, nodes))
-    target_x = (down * 2 + row // 16 - 1 + size_x) % size_x
-    target_y = (cross * 2 + (row // 4) % 4 - 1 + size_y) % size_y
-    target_z = depth * 2 + row % 4 - 1
-    inside = jnp.logical_and(target_z >= 0, target_z < size_z)
-    target = (target_x * size_y + target_y) * size_z + target_z
-    chosen = one_hot(jnp.logical_and(inside, lanes == target))
+        jnp.concatenate([moment_high, moment_low.astype(BF16)], axis=0), kernel_high[...]
+    )
+    near = wide_part[0:16] + wide_part[16:32] + matmul_turned(moment_high, kernel_low[...])
     near_high, rest = split(near)
     near_middle, near_low = split(rest)
     placed = matmul(
-        jnp.concatenate([near_high, near_middle, near_low.astype(BF16)], axis=0), chosen
+        jnp.concatenate([near_high, near_middle, near_low.astype(BF16)], axis=0), chosen[...]
     )
     node_out[...] = placed[0:16] + placed[16:32] + placed[32:48]
 
@@ -507,12 +514,17 @@
             entries.append(features[left] * features[right])
     for left in range(1, 5):
         entries.append(features[left] * features[left] * features[left])
-    model = jnp.zeros_like(density)
     for k, entry in enumerate(entries):
         terms[k : k + 1, :] = entry
-        model = model + coefficients[k] * entry
-    residual = friction - model
     table = terms[...]
+    model = lax.dot_general(
+        jnp.broadcast_to(coefficients[...], (8, TERMS)),
+        table,
+        (((1,), (0,)), ((), ())),
+        precision=lax.Precision.HIGHEST,
+        preferred_element_type=F32,
+    )
+    residual = friction - model[0:1]
     gram_out[...] = (
         lax.dot_general(
             table,
@@ -682,26 +694,32 @@
     own_speed, inner_speed = call(
         step_outside, [own, sums] + outside, (rows(32), rows(16)), contact_scratch(OUTSIDE, 3), "step_outside", 1 << 30
     )
-    inside_speed, outside_speed, sums = exchange(
+    table = jax.ShapeDtypeStruct((64, 8 * S), BF16)
+    inside_speed, outside_speed, weights = exchange(
         own_speed,
         inner_speed,
         4,
         False,
         lambda speed: call(
-            field_block, [own, speed], rows(72), contact_scratch(BLOCK, 9), "field_block", 1 << 31
+            functools.partial(field_weights, grid),
+            [own, speed, coefficients.reshape(1, TERMS)],
+            (
+                table,
+                table,
+                jax.ShapeDtypeStruct((64, nodes), BF16),
+                jax.ShapeDtypeStruct((1, TERMS), F32),
+            ),
+            [],
+            "field_weights",
+            1 << 30,
         ),
     )
     sums = call(
-        functools.partial(field_plane, len(inside)),
-        [sums] + inside + inside_speed,
-        rows(72),
-        contact_scratch(PLANE, 9),
-        "field_plane",
-        1 << 31,
+        field_inside, inside + inside_speed, rows(72), contact_scratch(INSIDE, 9), "field_inside", 1 << 31
     )
     force, partial = call(
-        functools.partial(field_outside, grid),
-        [own, own_speed, sums] + outside + outside_speed,
+        field_outside,
+        [own, own_speed, sums] + outside + outside_speed + list(weights[:3]),
         (rows(24), jax.ShapeDtypeStruct((16, nodes), F32)),
         [pltpu.VMEM((16, 8 * S), F32)] + contact_scratch(OUTSIDE, 9),
         "field_outside",
@@ -723,12 +741,12 @@
             jax.ShapeDtypeStruct((TERMS, TERMS), F32),
             jax.ShapeDtypeStruct((1, TERMS), F32),
         ),
-        in_specs=[SMEM_SPEC] + [VMEM_SPEC] * 4,
+        in_specs=[VMEM_SPEC] * 5,
         out_specs=(VMEM_SPEC,) * 5,
         scratch_shapes=[pltpu.VMEM((TERMS, nodes), F32)],
         compiler_params=params,
         name="library",
-    )(coefficients, partial, other, own_speed, force)
+    )(weights[3], partial, other, own_speed, force)
     return (velocity_new, force_next, residual_field, gram_matrix, moment.reshape(TERMS))
 
 

time: 47.9 us -> 45.8 us (0.956)
  waiting for transfers between devices: 16 us -> 11 us
  starting transfers between devices: 13.9 us -> 18 us
  Pallas kernels: 15.9 us -> 13.7 us
  local copies, waits for them, and re-layouts: 0.87 us -> 1.52 us
    ppermute x2, waiting for transfers between devices: 7.42 us -> 3.84 us  [body(): lax.ppermute(partial, 'down', [(i, i ^ distance) for i in range(down)])]
    ppermute x2, starting transfers between devices: 0.86 us -> 4.43 us  [body(): lax.ppermute(partial, 'down', [(i, i ^ distance) for i in range(down)])]
    ppermute x2, waiting for transfers between devices: 2.76 us -> 0.01 us  [exchange(): lax.ppermute(jnp.where(even, first, last), 'down', far)]
    pallas_call x5, Pallas kernels: 13 us -> 11.4 us  [call(): pl.pallas_call(kernel, out_shape=outputs, in_specs=[VMEM_SPEC] * len(inpu...]
    ppermute x1, waiting for transfers between devices: 0.01 us -> 1.33 us  [exchange(): side = lax.ppermute(own, 'cross', [(0, 1), (1, 0)])]
    unnamed x9, local copies, waits for them, and re-layouts: 0.81 us -> 1.46 us
    ppermute x2, starting transfers between devices: 5.51 us -> 6.06 us  [exchange(): lax.ppermute(jnp.where(even, first, last), 'down', far)]
    pallas_call x1, Pallas kernels: 1.47 us -> 0.94 us  [body(): pl.pallas_call(functools.partial(library_kernel, grid), out_shape=(vector...]
  transfers between devices with their start and end apart: 14 -> 14, of which waited for: 10 -> 10; matrix products, arithmetic and copies ran while one was open for 2% -> 2% of each run, Pallas kernels for 19% -> 17%
where the time goes in v2:
time: 45.8 us; the launch traced here: 45.1 us
  starting transfers between devices  18 us (39%)
  Pallas kernels  13.7 us (30%)
  waiting for transfers between devices  11 us (24%)
  local copies, waits for them, and re-layouts  1.52 us (3%)
  between operations  0.73 us (2%)
    pallas_call x5, Pallas kernels, call(): pl.pallas_call(kernel, out_shape=outputs, in_specs=[VMEM_SPEC] * len(inpu...  11.4 us
    ppermute x2, starting transfers between devices, exchange(): lax.ppermute(jnp.where(even, first, last), 'down', far)  6.06 us
    ppermute x2, starting transfers between devices, body(): lax.ppermute(partial, 'down', [(i, i ^ distance) for i in range(down)])  4.43 us
    ppermute x2, waiting for transfers between devices, body(): lax.ppermute(partial, 'down', [(i, i ^ distance) for i in range(down)])  3.84 us
    ppermute x1, starting transfers between devices, exchange(): lax.ppermute(jnp.concatenate([own, depth_halo], axis=0), 'cross', [(0, 1)...  2.89 us
    ppermute x2, starting transfers between devices, exchange(): depth_halo = lax.ppermute(inner, 'depth', [(0, 1), (1, 0)])  2.11 us
    ppermute x1, waiting for transfers between devices, exchange(): lax.ppermute(jnp.concatenate([own, depth_halo], axis=0), 'cross', [(0, 1)...  2.07 us
    ppermute x3, starting transfers between devices, shared(): lax.ppermute(value, axes, [(i, i ^ k) for i in range(peers)])  1.9 us
  transfers between devices with their start and end apart: 14, of which 10 were waited for; matrix products, arithmetic and copies ran while one was open for 2% of the time, Pallas kernels for 17%

profile of v2, /device:TPU:0, one launch (start us, length us, event | category | flops | bytes accessed | tf_op | source)
XLA Modules:
  0.0 45.1 jit_solution(2395312821221596245)
XLA Ops:
  0.6 1.4 %pack.1 = (f32[64,128]{1,0:T(8,128)}, f32[32,128]{1,0:T(8,128)}) custom-call(s32[2,2,2]{2,1,0:T(2,128)} %counts_hbm.1, f32[3,2,2,2,128]{4,3,2,1,0:T(2,128)} %positions_hbm.1, f32[3,2,2,2,128]{4,3,2,1,0:T(2,128)} %velocities_hbm.1, f32[2,2,2,128]{3,2,1,0:T(2,128)} %radii_hbm.1), custom_call_target="tpu_custom_call" | custom-call | tf_op jit(solution)/shard_map/pack/pallas_call | solution.py:677
  2.0 0.5 %collective-permute-start = (f32[32,128]{1,0:T(8,128)}, f32[32,128]{1,0:T(8,128)S(1)}, u32[]{:S(2)}, u32[]{:S(2)}) collective-permute-start(f32[32,128]{1,0:T(8,128)} %get-tuple-element.29), channel_id=1, source_target_pairs={{0,1},{1,0},{2,3},{3,2},{4,5},{5,4},{6,7},{7,6},{8,9},{9,8},{10,11... | collective-permute-start | bytes 49160 | tf_op jit(solution)/shard_map/ppermute | solution.py:575
  2.6 0.8 %constant_dynamic-update-slice_fusion.11 = (f32[96,128]{1,0:T(8,128)S(1)}, f32[96,128]{1,0:T(8,128)S(1)}) fusion(f32[64,128]{1,0:T(8,128)} %get-tuple-element.28.refs_0_.own), kind=kLoop, calls=%fused_computation.12 | loop fusion | bytes 65536
  3.4 0.3 collective-permute-done.refs_1_
  3.6 2.9 %collective-permute-start.1 = (f32[96,128]{1,0:T(8,128)S(1)}, f32[96,128]{1,0:T(8,128)S(1)}, u32[]{:S(2)}, u32[]{:S(2)}) collective-permute-start(f32[96,128]{1,0:T(8,128)S(1)} %pad_maximum_fusion), channel_id=1, source_target_pairs={{0,2},{2,0},{1,3},{3,1},{4,6},{6,4},{5,7},{7,5},{8,10},{10,8},{9,1... | collective-permute-start | bytes 147464 | tf_op jit(solution)/shard_map/ppermute | solution.py:578
  6.5 2.1 %collective-permute-done.1.refs_2_ = f32[96,128]{1,0:T(8,128)S(1)} collective-permute-done((f32[96,128]{1,0:T(8,128)S(1)}, f32[96,128]{1,0:T(8,128)S(1)}, u32[]{:S(2)}, u32[]{:S(2)}) %collective-permute-start.1) | collective-permute-done | bytes 49184 | tf_op jit(solution)/shard_map/ppermute | solution.py:578
  8.6 4.2 %collective-permute-start.3 = (f32[96,128]{1,0:T(8,128)S(1)}, f32[96,128]{1,0:T(8,128)S(1)}, u32[]{:S(2)}, u32[]{:S(2)}) collective-permute-start(f32[96,128]{1,0:T(8,128)S(1)} %get-tuple-element.51), channel_id=1, source_target_pairs={{0,12},{4,8},{8,4},{12,0},{1,13},{5,9},{9,5},{13,1},{2,14},{6,10},... | collective-permute-start | bytes 147464 | tf_op jit(solution)/shard_map/ppermute | solution.py:631
  12.8 0.0 collective-permute-start.2
  12.8 3.3 %step_inside.1.sums_in = f32[24,128]{1,0:T(8,128)S(1)} custom-call(f32[64,128]{1,0:T(8,128)S(1)} %copy-done, f32[32,128]{1,0:T(8,128)S(1)} %collective-permute-done.refs_1_, f32[96,128]{1,0:T(8,128)S(1)} %collective-permute-done.1.refs_2_), custom_call_target="tpu_custom_call" | custom-call | flops 2147483648 | bytes 1048576 | tf_op jit(solution)/shard_map/step_inside/pallas_call | solution.py:666
  16.2 0.7 %collective-permute-done.2.near.near_old = f32[96,128]{1,0:T(8,128)S(1)} collective-permute-done((f32[96,128]{1,0:T(8,128)S(1)}, f32[96,128]{1,0:T(8,128)S(1)}, u32[]{:S(2)}, u32[]{:S(2)}) %collective-permute-start.2) | collective-permute-done | bytes 49184 | tf_op jit(solution)/shard_map/ppermute | solution.py:630
  16.9 1.6 %step_outside.1 = (f32[32,128]{1,0:T(8,128)S(1)}, f32[16,128]{1,0:T(8,128)S(1)}) custom-call(f32[64,128]{1,0:T(8,128)S(1)} %copy-done, f32[24,128]{1,0:T(8,128)S(1)} %step_inside.1.sums_in, f32[96,128]{1,0:T(8,128)S(1)} %collective-permute-done.2.near.near_old, f32[96,128]{1,0:T(8,128)S(1)} %collective-permute-done.3.far.far_old), custom_call_target="tpu_custom_call" | custom-call | flops 1073741824 | bytes 1048576 | tf_op jit(solution)/shard_map/step_outside/pallas_call | solution.py:666
  18.5 0.1 collective-permute-start.6
  18.5 1.6 %collective-permute-start.4 = (f32[16,128]{1,0:T(8,128)S(1)}, f32[16,128]{1,0:T(8,128)S(1)}, u32[]{:S(2)}, u32[]{:S(2)}) collective-permute-start(f32[16,128]{1,0:T(8,128)S(1)} %get-tuple-element.31), channel_id=1, source_target_pairs={{0,1},{1,0},{2,3},{3,2},{4,5},{5,4},{6,7},{7,6},{8,9},{9,8},{10,11... | collective-permute-start | bytes 24584 | tf_op jit(solution)/shard_map/ppermute | solution.py:575
  20.1 0.5 %collective-permute-start.5 = (f32[32,128]{1,0:T(8,128)S(1)}, f32[32,128]{1,0:T(8,128)S(1)}, u32[]{:S(2)}, u32[]{:S(2)}) collective-permute-start(f32[32,128]{1,0:T(8,128)S(1)} %get-tuple-element.32.own_speed.refs_3_.speed), channel_id=1, source_target_pairs={{0,2},{2,0},{1,3},{3,1},{4,6},{6,4},{5,7},{7,5},{8,10},{10,8},{9,1... | collective-permute-start | bytes 49160 | tf_op jit(solution)/shard_map/ppermute | solution.py:584
  20.7 0.3 collective-permute-done.4.refs_4_
  21.0 0.7 %collective-permute-done.6.refs_6_ = f32[16,128]{1,0:T(8,128)S(1)} collective-permute-done((f32[16,128]{1,0:T(8,128)S(1)}, f32[16,128]{1,0:T(8,128)S(1)}, u32[]{:S(2)}, u32[]{:S(2)}) %collective-permute-start.6) | collective-permute-done | bytes 8224 | tf_op jit(solution)/shard_map/ppermute | solution.py:585
  21.6 0.7 %copy-done.1 = f32[48]{0:T(128)S(1)} copy-done((f32[48]{0:T(128)S(1)}, f32[48]{0:T(128)}, u32[]{:S(2)}) %copy-start.1) | copy-done | bytes 216
  22.3 0.2 field_weights.1
  22.5 1.3 %collective-permute-done.5.refs_5_ = f32[32,128]{1,0:T(8,128)S(1)} collective-permute-done((f32[32,128]{1,0:T(8,128)S(1)}, f32[32,128]{1,0:T(8,128)S(1)}, u32[]{:S(2)}, u32[]{:S(2)}) %collective-permute-start.5) | collective-permute-done | bytes 16416 | tf_op jit(solution)/shard_map/ppermute | solution.py:584
  23.9 1.9 %collective-permute-start.8 = (f32[48,128]{1,0:T(8,128)S(1)}, f32[48,128]{1,0:T(8,128)S(1)}, u32[]{:S(2)}, u32[]{:S(2)}) collective-permute-start(f32[48,128]{1,0:T(8,128)S(1)} %get-tuple-element.53), channel_id=1, source_target_pairs={{0,12},{4,8},{8,4},{12,0},{1,13},{5,9},{9,5},{13,1},{2,14},{6,10},... | collective-permute-start | bytes 73736 | tf_op jit(solution)/shard_map/ppermute | solution.py:631
  25.8 4.3 %field_inside.1.sums_in = f32[72,128]{1,0:T(8,128)S(1)} custom-call(f32[64,128]{1,0:T(8,128)S(1)} %copy-done, f32[32,128]{1,0:T(8,128)S(1)} %collective-permute-done.refs_1_, f32[96,128]{1,0:T(8,128)S(1)} %collective-permute-done.1.refs_2_, f32[32,128]{1,0:T(8,128)S(1)} %get-tuple-element.32.own_speed.refs_3_.speed, ...), custom_call_target="tpu_custom_call" | custom-call | flops 2147483648 | bytes 1048576 | tf_op jit(solution)/shard_map/field_inside/pallas_call | solution.py:666
  30.1 2.0 %field_outside.1 = (f32[24,128]{1,0:T(8,128)S(1)}, f32[16,128]{1,0:T(8,128)S(1)}) custom-call(f32[64,128]{1,0:T(8,128)S(1)} %copy-done, f32[32,128]{1,0:T(8,128)S(1)} %get-tuple-element.32.own_speed.refs_3_.speed, f32[72,128]{1,0:T(8,128)S(1)} %field_inside.1.sums_in, f32[96,128]{1,0:T(8,128)S(1)} %collective-permute-done.2.near.near_old, ...), custom_call_target="tpu_custom_call" | custom-call | flops 1073741824 | bytes 1048576 | tf_op jit(solution)/shard_map/field_outside/pallas_call | solution.py:666
  32.1 0.4 collective-permute-start.10
  32.5 1.5 %collective-permute-start.9 = (f32[16,128]{1,0:T(8,128)S(1)}, f32[16,128]{1,0:T(8,128)S(1)}, u32[]{:S(2)}, u32[]{:S(2)}) collective-permute-start(f32[16,128]{1,0:T(8,128)S(1)} %get-tuple-element.44), channel_id=1, source_target_pairs={{0,1},{1,0},{2,3},{3,2},{4,5},{5,4},{6,7},{7,6},{8,9},{9,8},{10,11... | collective-permute-start | bytes 24584 | tf_op jit(solution)/shard_map/ppermute | solution.py:645
  34.0 1.2 %collective-permute-done.11 = f32[16,128]{1,0:T(8,128)S(1)} collective-permute-done((f32[16,128]{1,0:T(8,128)S(1)}, f32[16,128]{1,0:T(8,128)S(1)}, u32[]{:S(2)}, u32[]{:S(2)}) %collective-permute-start.11) | collective-permute-done | bytes 8224 | tf_op jit(solution)/shard_map/ppermute | solution.py:645
  35.2 0.6 %collective-permute-done.10 = f32[16,128]{1,0:T(8,128)S(1)} collective-permute-done((f32[16,128]{1,0:T(8,128)S(1)}, f32[16,128]{1,0:T(8,128)S(1)}, u32[]{:S(2)}, u32[]{:S(2)}) %collective-permute-start.10) | collective-permute-done | bytes 8224 | tf_op jit(solution)/shard_map/ppermute | solution.py:645
  35.8 0.0 collective-permute-done.9
  35.8 2.1 %collective-permute-start.12 = (f32[16,128]{1,0:T(8,128)S(1)}, f32[16,128]{1,0:T(8,128)S(1)}, u32[]{:S(2)}, u32[]{:S(2)}) collective-permute-start(f32[16,128]{1,0:T(8,128)S(1)} %add_add_fusion), channel_id=1, source_target_pairs={{0,4},{4,0},{8,12},{12,8},{1,5},{5,1},{9,13},{13,9},{2,6},{6,2},{1... | collective-permute-start | bytes 24584 | tf_op jit(solution)/shard_map/ppermute | solution.py:731
  37.9 1.6 %collective-permute-done.12 = f32[16,128]{1,0:T(8,128)S(1)} collective-permute-done((f32[16,128]{1,0:T(8,128)S(1)}, f32[16,128]{1,0:T(8,128)S(1)}, u32[]{:S(2)}, u32[]{:S(2)}) %collective-permute-start.12) | collective-permute-done | bytes 8224 | tf_op jit(solution)/shard_map/ppermute | solution.py:731
  39.6 2.4 %collective-permute-start.13 = (f32[16,128]{1,0:T(8,128)S(1)}, f32[16,128]{1,0:T(8,128)S(1)}, u32[]{:S(2)}, u32[]{:S(2)}) collective-permute-start(f32[16,128]{1,0:T(8,128)S(1)} %add.15.mine), channel_id=1, source_target_pairs={{0,8},{4,12},{8,0},{12,4},{1,9},{5,13},{9,1},{13,5},{2,10},{6,14},... | collective-permute-start | bytes 24584 | tf_op jit(solution)/shard_map/ppermute | solution.py:731
  41.9 2.2 %collective-permute-done.13.other = f32[16,128]{1,0:T(8,128)S(1)} collective-permute-done((f32[16,128]{1,0:T(8,128)S(1)}, f32[16,128]{1,0:T(8,128)S(1)}, u32[]{:S(2)}, u32[]{:S(2)}) %collective-permute-start.13) | collective-permute-done | bytes 8224 | tf_op jit(solution)/shard_map/ppermute | solution.py:731
  44.1 0.9 %library.1 = (f32[3,2,2,2,128]{4,3,2,1,0:T(2,128)}, f32[3,2,2,2,128]{4,3,2,1,0:T(2,128)}, f32[2,2,2]{2,1,0:T(2,128)}, f32[48,48]{1,0:T(8,128)}, f32[1,48]{1,0:T(1,128)}) custom-call(f32[1,48]{1,0:T(1,128)S(1)} %get-tuple-element.37.coefficients, f32[16,128]{1,0:T(8,128)S(1)} %add.15.mine, f32[16,128]{1,0:T(8,128)S(1)} %collective-permute-done.13.other, ...), custom_call_target="tpu_custom_call" | custom-call | tf_op jit(solution)/shard_map/library/pallas_call | solution.py:735
  (24 shorter events, 0.1 us)
Async XLA Ops:
  2.0 1.6 %collective-permute-start = (f32[32,128]{1,0:T(8,128)}, f32[32,128]{1,0:T(8,128)S(1)}, u32[]{:S(2)}, u32[]{:S(2)}) collective-permute-start(f32[32,128]{1,0:T(8,128)} %get-tuple-element.29), channel_id=1, source_target_pairs={{0,1},{1,0},{2,3},{3,2},{4,5},{5,4},{6,7},{7,6},{8,9},{9,8},{10,11... | collective-permute-start | bytes 49160 | tf_op jit(solution)/shard_map/ppermute | solution.py:575
  2.6 1.1 %copy-start = (f32[64,128]{1,0:T(8,128)S(1)}, f32[64,128]{1,0:T(8,128)}, u32[]{:S(2)}) copy-start(f32[64,128]{1,0:T(8,128)} %get-tuple-element.28.refs_0_.own) | copy-start | bytes 98308
  3.6 5.0 %collective-permute-start.1 = (f32[96,128]{1,0:T(8,128)S(1)}, f32[96,128]{1,0:T(8,128)S(1)}, u32[]{:S(2)}, u32[]{:S(2)}) collective-permute-start(f32[96,128]{1,0:T(8,128)S(1)} %pad_maximum_fusion), channel_id=1, source_target_pairs={{0,2},{2,0},{1,3},{3,1},{4,6},{6,4},{5,7},{7,5},{8,10},{10,8},{9,1... | collective-permute-start | bytes 147464 | tf_op jit(solution)/shard_map/ppermute | solution.py:578
  8.6 7.5 %collective-permute-start.3 = (f32[96,128]{1,0:T(8,128)S(1)}, f32[96,128]{1,0:T(8,128)S(1)}, u32[]{:S(2)}, u32[]{:S(2)}) collective-permute-start(f32[96,128]{1,0:T(8,128)S(1)} %get-tuple-element.51), channel_id=1, source_target_pairs={{0,12},{4,8},{8,4},{12,0},{1,13},{5,9},{9,5},{13,1},{2,14},{6,10},... | collective-permute-start | bytes 147464 | tf_op jit(solution)/shard_map/ppermute | solution.py:631
  12.8 4.1 %collective-permute-start.2 = (f32[96,128]{1,0:T(8,128)S(1)}, f32[96,128]{1,0:T(8,128)S(1)}, u32[]{:S(2)}, u32[]{:S(2)}) collective-permute-start(f32[96,128]{1,0:T(8,128)S(1)} %get-tuple-element.52), channel_id=1, source_target_pairs={{0,4},{4,0},{8,12},{12,8},{1,5},{5,1},{9,13},{13,9},{2,6},{6,2},{1... | collective-permute-start | bytes 147464 | tf_op jit(solution)/shard_map/ppermute | solution.py:630
  18.5 3.2 %collective-permute-start.6 = (f32[16,128]{1,0:T(8,128)S(1)}, f32[16,128]{1,0:T(8,128)S(1)}, u32[]{:S(2)}, u32[]{:S(2)}) collective-permute-start(f32[16,128]{1,0:T(8,128)S(1)} %get-tuple-element.31), channel_id=1, source_target_pairs={{0,3},{1,2},{2,1},{3,0},{4,7},{5,6},{6,5},{7,4},{8,11},{9,10},{10,... | collective-permute-start | bytes 24584 | tf_op jit(solution)/shard_map/ppermute | solution.py:585
  18.5 2.4 %collective-permute-start.4 = (f32[16,128]{1,0:T(8,128)S(1)}, f32[16,128]{1,0:T(8,128)S(1)}, u32[]{:S(2)}, u32[]{:S(2)}) collective-permute-start(f32[16,128]{1,0:T(8,128)S(1)} %get-tuple-element.31), channel_id=1, source_target_pairs={{0,1},{1,0},{2,3},{3,2},{4,5},{5,4},{6,7},{7,6},{8,9},{9,8},{10,11... | collective-permute-start | bytes 24584 | tf_op jit(solution)/shard_map/ppermute | solution.py:575
  20.1 3.7 %collective-permute-start.5 = (f32[32,128]{1,0:T(8,128)S(1)}, f32[32,128]{1,0:T(8,128)S(1)}, u32[]{:S(2)}, u32[]{:S(2)}) collective-permute-start(f32[32,128]{1,0:T(8,128)S(1)} %get-tuple-element.32.own_speed.refs_3_.speed), channel_id=1, source_target_pairs={{0,2},{2,0},{1,3},{3,1},{4,6},{6,4},{5,7},{7,5},{8,10},{10,8},{9,1... | collective-permute-start | bytes 49160 | tf_op jit(solution)/shard_map/ppermute | solution.py:584
  21.6 0.7 %copy-start.1 = (f32[48]{0:T(128)S(1)}, f32[48]{0:T(128)}, u32[]{:S(2)}) copy-start(f32[48]{0:T(128)} %param.9) | copy-start | bytes 580
  23.9 6.2 %collective-permute-start.8 = (f32[48,128]{1,0:T(8,128)S(1)}, f32[48,128]{1,0:T(8,128)S(1)}, u32[]{:S(2)}, u32[]{:S(2)}) collective-permute-start(f32[48,128]{1,0:T(8,128)S(1)} %get-tuple-element.53), channel_id=1, source_target_pairs={{0,12},{4,8},{8,4},{12,0},{1,13},{5,9},{9,5},{13,1},{2,14},{6,10},... | collective-permute-start | bytes 73736 | tf_op jit(solution)/shard_map/ppermute | solution.py:631
  25.8 4.3 %collective-permute-start.7 = (f32[48,128]{1,0:T(8,128)S(1)}, f32[48,128]{1,0:T(8,128)S(1)}, u32[]{:S(2)}, u32[]{:S(2)}) collective-permute-start(f32[48,128]{1,0:T(8,128)S(1)} %get-tuple-element.54), channel_id=1, source_target_pairs={{0,4},{4,0},{8,12},{12,8},{1,5},{5,1},{9,13},{13,9},{2,6},{6,2},{1... | collective-permute-start | bytes 73736 | tf_op jit(solution)/shard_map/ppermute | solution.py:630
  32.1 3.1 %collective-permute-start.11 = (f32[16,128]{1,0:T(8,128)S(1)}, f32[16,128]{1,0:T(8,128)S(1)}, u32[]{:S(2)}, u32[]{:S(2)}) collective-permute-start(f32[16,128]{1,0:T(8,128)S(1)} %get-tuple-element.44), channel_id=1, source_target_pairs={{0,3},{1,2},{2,1},{3,0},{4,7},{5,6},{6,5},{7,4},{8,11},{9,10},{10,... | collective-permute-start | bytes 24584 | tf_op jit(solution)/shard_map/ppermute | solution.py:645
  32.1 3.7 %collective-permute-start.10 = (f32[16,128]{1,0:T(8,128)S(1)}, f32[16,128]{1,0:T(8,128)S(1)}, u32[]{:S(2)}, u32[]{:S(2)}) collective-permute-start(f32[16,128]{1,0:T(8,128)S(1)} %get-tuple-element.44), channel_id=1, source_target_pairs={{0,2},{1,3},{2,0},{3,1},{4,6},{5,7},{6,4},{7,5},{8,10},{9,11},{10,... | collective-permute-start | bytes 24584 | tf_op jit(solution)/shard_map/ppermute | solution.py:645
  32.5 3.4 %collective-permute-start.9 = (f32[16,128]{1,0:T(8,128)S(1)}, f32[16,128]{1,0:T(8,128)S(1)}, u32[]{:S(2)}, u32[]{:S(2)}) collective-permute-start(f32[16,128]{1,0:T(8,128)S(1)} %get-tuple-element.44), channel_id=1, source_target_pairs={{0,1},{1,0},{2,3},{3,2},{4,5},{5,4},{6,7},{7,6},{8,9},{9,8},{10,11... | collective-permute-start | bytes 24584 | tf_op jit(solution)/shard_map/ppermute | solution.py:645
  35.8 3.7 %collective-permute-start.12 = (f32[16,128]{1,0:T(8,128)S(1)}, f32[16,128]{1,0:T(8,128)S(1)}, u32[]{:S(2)}, u32[]{:S(2)}) collective-permute-start(f32[16,128]{1,0:T(8,128)S(1)} %add_add_fusion), channel_id=1, source_target_pairs={{0,4},{4,0},{8,12},{12,8},{1,5},{5,1},{9,13},{13,9},{2,6},{6,2},{1... | collective-permute-start | bytes 24584 | tf_op jit(solution)/shard_map/ppermute | solution.py:731
  39.6 4.5 %collective-permute-start.13 = (f32[16,128]{1,0:T(8,128)S(1)}, f32[16,128]{1,0:T(8,128)S(1)}, u32[]{:S(2)}, u32[]{:S(2)}) collective-permute-start(f32[16,128]{1,0:T(8,128)S(1)} %add.15.mine), channel_id=1, source_target_pairs={{0,8},{4,12},{8,0},{12,4},{1,9},{5,13},{9,1},{13,5},{2,10},{6,14},... | collective-permute-start | bytes 24584 | tf_op jit(solution)/shard_map/ppermute | solution.py:731

commit v3 on v2

--- a/solution.py
+++ b/solution.py
@@ -435,7 +435,7 @@
 
 
 def library_kernel(
-    grid, coefficients, mine, other, speed, force, velocity_out, force_out, residual_out, gram_out, moment_out, terms
+    grid, coefficients, parts, speed, force, velocity_out, force_out, residual_out, gram_out, moment_out, terms
 ):
     flat = lax.axis_index("depth") == 0
     for k in range(3):
@@ -447,7 +447,7 @@
                 for z in range(2):
                     velocity_out[k, a, b, z : z + 1, :] = jnp.where(flat, layers[z], layers[1 - z])
                     force_out[k, a, b, z : z + 1, :] = jnp.where(flat, pulls[z], pulls[1 - z])
-    fields = mine[...] + other[...]
+    fields = jnp.sum(parts[...], axis=0)
     size_x, size_y, size_z = grid
     nodes = size_x * size_y * size_z
     lanes = lax.broadcasted_iota(jnp.int32, (1, nodes), 1)
@@ -572,6 +572,8 @@
     def cells(block, first, count):
         return block[first * height : (first + count) * height]
 
+    if cross == 2 and not joined:
+        side = lax.ppermute(own, "cross", [(0, 1), (1, 0)])
     depth_halo = lax.ppermute(inner, "depth", [(0, 1), (1, 0)])
     if cross == 2:
         if joined:
@@ -581,7 +583,6 @@
             diag = cells(side, 8, 4)
             sides = [side]
         else:
-            side = lax.ppermute(own, "cross", [(0, 1), (1, 0)])
             diag = lax.ppermute(inner, ("cross", "depth"), [(i, 3 - i) for i in range(4)])
             sides = [side, diag]
 
@@ -726,12 +727,7 @@
         1 << 30,
     )
     partial = tree_sum(shared(partial, ("cross", "depth"), cross * depth))
-    distance = 1
-    while distance < down:
-        other = lax.ppermute(partial, "down", [(i, i ^ distance) for i in range(down)])
-        distance = distance * 2
-        if distance < down:
-            partial = partial + other
+    parts = lax.all_to_all(jnp.broadcast_to(partial, (down, 16, nodes)), "down", 0, 0)
     velocity_new, force_next, residual_field, gram_matrix, moment = pl.pallas_call(
         functools.partial(library_kernel, grid),
         out_shape=(
@@ -741,12 +737,12 @@
             jax.ShapeDtypeStruct((TERMS, TERMS), F32),
             jax.ShapeDtypeStruct((1, TERMS), F32),
         ),
-        in_specs=[VMEM_SPEC] * 5,
+        in_specs=[VMEM_SPEC] * 4,
         out_specs=(VMEM_SPEC,) * 5,
         scratch_shapes=[pltpu.VMEM((TERMS, nodes), F32)],
         compiler_params=params,
         name="library",
-    )(weights[3], partial, other, own_speed, force)
+    )(weights[3], parts, own_speed, force)
     return (velocity_new, force_next, residual_field, gram_matrix, moment.reshape(TERMS))
 
 

time: 45.8 us -> 45.9 us (level)
  blocking collectives: 0 us -> 9 us
  starting transfers between devices: 18 us -> 13.6 us
  waiting for transfers between devices: 11 us -> 7.51 us
  Pallas kernels: 13.7 us -> 13.2 us
    all_to_all x0 -> x1, blocking collectives: none -> 9 us  [body(): lax.all_to_all(jnp.broadcast_to(partial, (down, 16, nodes)), 'down', 0, 0)]
    ppermute x2 -> x0, starting transfers between devices: 4.43 us -> none  [body(): lax.ppermute(partial, 'down', [(i, i ^ distance) for i in range(down)])]
    ppermute x2 -> x0, waiting for transfers between devices: 3.84 us -> none  [body(): lax.ppermute(partial, 'down', [(i, i ^ distance) for i in range(down)])]
    pallas_call x5, Pallas kernels: 11.4 us -> 10.8 us  [call(): pl.pallas_call(kernel, out_shape=outputs, in_specs=[VMEM_SPEC] * len(inpu...]
  transfers between devices with their start and end apart: 14 -> 12, of which waited for: 10 -> 10; matrix products, arithmetic and copies ran while one was open for 2% -> 2% of each run, Pallas kernels for 17% -> 16%
where the time goes in v3:
time: 45.9 us; the launch traced here: 45.5 us
  starting transfers between devices  13.6 us (30%)
  Pallas kernels  13.2 us (29%)
  blocking collectives  9 us (20%)
  waiting for transfers between devices  7.51 us (16%)
  local copies, waits for them, and re-layouts  1.52 us (3%)
  between operations  0.72 us (2%)
    pallas_call x5, Pallas kernels, call(): pl.pallas_call(kernel, out_shape=outputs, in_specs=[VMEM_SPEC] * len(inpu...  10.8 us
    all_to_all x1, blocking collectives, body(): lax.all_to_all(jnp.broadcast_to(partial, (down, 16, nodes)), 'down', 0, 0)  9 us
    ppermute x2, starting transfers between devices, exchange(): lax.ppermute(jnp.where(even, first, last), 'down', far)  6.06 us
    ppermute x1, starting transfers between devices, exchange(): lax.ppermute(jnp.concatenate([own, depth_halo], axis=0), 'cross', [(0, 1)...  2.89 us
    ppermute x2, starting transfers between devices, exchange(): depth_halo = lax.ppermute(inner, 'depth', [(0, 1), (1, 0)])  2.11 us
    ppermute x1, waiting for transfers between devices, exchange(): lax.ppermute(jnp.concatenate([own, depth_halo], axis=0), 'cross', [(0, 1)...  2.07 us
    ppermute x3, starting transfers between devices, shared(): lax.ppermute(value, axes, [(i, i ^ k) for i in range(peers)])  1.93 us
    ppermute x3, waiting for transfers between devices, shared(): lax.ppermute(value, axes, [(i, i ^ k) for i in range(peers)])  1.81 us
  transfers between devices with their start and end apart: 12, of which 10 were waited for; matrix products, arithmetic and copies ran while one was open for 2% of the time, Pallas kernels for 16%

profile of v3, /device:TPU:0, one launch (start us, length us, event | category | flops | bytes accessed | tf_op | source)
XLA Modules:
  0.0 45.5 jit_solution(12863742667426681702)
XLA Ops:
  0.6 1.4 %pack.1 = (f32[64,128]{1,0:T(8,128)}, f32[32,128]{1,0:T(8,128)}) custom-call(s32[2,2,2]{2,1,0:T(2,128)} %counts_hbm.1, f32[3,2,2,2,128]{4,3,2,1,0:T(2,128)} %positions_hbm.1, f32[3,2,2,2,128]{4,3,2,1,0:T(2,128)} %velocities_hbm.1, f32[2,2,2,128]{3,2,1,0:T(2,128)} %radii_hbm.1), custom_call_target="tpu_custom_call" | custom-call | tf_op jit(solution)/shard_map/pack/pallas_call | solution.py:678
  2.0 0.5 %collective-permute-start = (f32[32,128]{1,0:T(8,128)}, f32[32,128]{1,0:T(8,128)S(1)}, u32[]{:S(2)}, u32[]{:S(2)}) collective-permute-start(f32[32,128]{1,0:T(8,128)} %get-tuple-element.29), channel_id=1, source_target_pairs={{0,1},{1,0},{2,3},{3,2},{4,5},{5,4},{6,7},{7,6},{8,9},{9,8},{10,11... | collective-permute-start | bytes 49160 | tf_op jit(solution)/shard_map/ppermute | solution.py:577
  2.6 0.8 %constant_dynamic-update-slice_fusion.11 = (f32[96,128]{1,0:T(8,128)S(1)}, f32[96,128]{1,0:T(8,128)S(1)}) fusion(f32[64,128]{1,0:T(8,128)} %get-tuple-element.28.refs_0_.own), kind=kLoop, calls=%fused_computation.12 | loop fusion | bytes 65536
  3.4 0.3 collective-permute-done.refs_1_
  3.6 2.9 %collective-permute-start.1 = (f32[96,128]{1,0:T(8,128)S(1)}, f32[96,128]{1,0:T(8,128)S(1)}, u32[]{:S(2)}, u32[]{:S(2)}) collective-permute-start(f32[96,128]{1,0:T(8,128)S(1)} %pad_maximum_fusion), channel_id=1, source_target_pairs={{0,2},{2,0},{1,3},{3,1},{4,6},{6,4},{5,7},{7,5},{8,10},{10,8},{9,1... | collective-permute-start | bytes 147464 | tf_op jit(solution)/shard_map/ppermute | solution.py:580
  6.5 2.1 %collective-permute-done.1.refs_2_ = f32[96,128]{1,0:T(8,128)S(1)} collective-permute-done((f32[96,128]{1,0:T(8,128)S(1)}, f32[96,128]{1,0:T(8,128)S(1)}, u32[]{:S(2)}, u32[]{:S(2)}) %collective-permute-start.1) | collective-permute-done | bytes 49184 | tf_op jit(solution)/shard_map/ppermute | solution.py:580
  8.6 4.2 %collective-permute-start.3 = (f32[96,128]{1,0:T(8,128)S(1)}, f32[96,128]{1,0:T(8,128)S(1)}, u32[]{:S(2)}, u32[]{:S(2)}) collective-permute-start(f32[96,128]{1,0:T(8,128)S(1)} %get-tuple-element.51), channel_id=1, source_target_pairs={{0,12},{4,8},{8,4},{12,0},{1,13},{5,9},{9,5},{13,1},{2,14},{6,10},... | collective-permute-start | bytes 147464 | tf_op jit(solution)/shard_map/ppermute | solution.py:632
  12.8 0.0 collective-permute-start.2
  12.8 3.3 %step_inside.1.sums_in = f32[24,128]{1,0:T(8,128)S(1)} custom-call(f32[64,128]{1,0:T(8,128)S(1)} %copy-done, f32[32,128]{1,0:T(8,128)S(1)} %collective-permute-done.refs_1_, f32[96,128]{1,0:T(8,128)S(1)} %collective-permute-done.1.refs_2_), custom_call_target="tpu_custom_call" | custom-call | flops 2147483648 | bytes 1048576 | tf_op jit(solution)/shard_map/step_inside/pallas_call | solution.py:667
  16.2 0.7 %collective-permute-done.2.near.near_old = f32[96,128]{1,0:T(8,128)S(1)} collective-permute-done((f32[96,128]{1,0:T(8,128)S(1)}, f32[96,128]{1,0:T(8,128)S(1)}, u32[]{:S(2)}, u32[]{:S(2)}) %collective-permute-start.2) | collective-permute-done | bytes 49184 | tf_op jit(solution)/shard_map/ppermute | solution.py:631
  16.9 1.6 %step_outside.1 = (f32[32,128]{1,0:T(8,128)S(1)}, f32[16,128]{1,0:T(8,128)S(1)}) custom-call(f32[64,128]{1,0:T(8,128)S(1)} %copy-done, f32[24,128]{1,0:T(8,128)S(1)} %step_inside.1.sums_in, f32[96,128]{1,0:T(8,128)S(1)} %collective-permute-done.2.near.near_old, f32[96,128]{1,0:T(8,128)S(1)} %collective-permute-done.3.far.far_old), custom_call_target="tpu_custom_call" | custom-call | flops 1073741824 | bytes 1048576 | tf_op jit(solution)/shard_map/step_outside/pallas_call | solution.py:667
  18.5 0.1 collective-permute-start.6
  18.5 1.6 %collective-permute-start.4 = (f32[16,128]{1,0:T(8,128)S(1)}, f32[16,128]{1,0:T(8,128)S(1)}, u32[]{:S(2)}, u32[]{:S(2)}) collective-permute-start(f32[16,128]{1,0:T(8,128)S(1)} %get-tuple-element.31), channel_id=1, source_target_pairs={{0,1},{1,0},{2,3},{3,2},{4,5},{5,4},{6,7},{7,6},{8,9},{9,8},{10,11... | collective-permute-start | bytes 24584 | tf_op jit(solution)/shard_map/ppermute | solution.py:577
  20.1 0.5 %collective-permute-start.5 = (f32[32,128]{1,0:T(8,128)S(1)}, f32[32,128]{1,0:T(8,128)S(1)}, u32[]{:S(2)}, u32[]{:S(2)}) collective-permute-start(f32[32,128]{1,0:T(8,128)S(1)} %get-tuple-element.32.own_speed.refs_3_.speed), channel_id=1, source_target_pairs={{0,2},{2,0},{1,3},{3,1},{4,6},{6,4},{5,7},{7,5},{8,10},{10,8},{9,1... | collective-permute-start | bytes 49160 | tf_op jit(solution)/shard_map/ppermute | solution.py:576
  20.7 0.3 collective-permute-done.4.refs_4_
  21.0 0.7 %collective-permute-done.6.refs_6_ = f32[16,128]{1,0:T(8,128)S(1)} collective-permute-done((f32[16,128]{1,0:T(8,128)S(1)}, f32[16,128]{1,0:T(8,128)S(1)}, u32[]{:S(2)}, u32[]{:S(2)}) %collective-permute-start.6) | collective-permute-done | bytes 8224 | tf_op jit(solution)/shard_map/ppermute | solution.py:586
  21.6 0.7 %copy-done.1 = f32[48]{0:T(128)S(1)} copy-done((f32[48]{0:T(128)S(1)}, f32[48]{0:T(128)}, u32[]{:S(2)}) %copy-start.1) | copy-done | bytes 216
  22.3 0.2 field_weights.1
  22.5 1.3 %collective-permute-done.5.refs_5_ = f32[32,128]{1,0:T(8,128)S(1)} collective-permute-done((f32[32,128]{1,0:T(8,128)S(1)}, f32[32,128]{1,0:T(8,128)S(1)}, u32[]{:S(2)}, u32[]{:S(2)}) %collective-permute-start.5) | collective-permute-done | bytes 16416 | tf_op jit(solution)/shard_map/ppermute | solution.py:576
  23.9 1.9 %collective-permute-start.8 = (f32[48,128]{1,0:T(8,128)S(1)}, f32[48,128]{1,0:T(8,128)S(1)}, u32[]{:S(2)}, u32[]{:S(2)}) collective-permute-start(f32[48,128]{1,0:T(8,128)S(1)} %get-tuple-element.53), channel_id=1, source_target_pairs={{0,12},{4,8},{8,4},{12,0},{1,13},{5,9},{9,5},{13,1},{2,14},{6,10},... | collective-permute-start | bytes 73736 | tf_op jit(solution)/shard_map/ppermute | solution.py:632
  25.8 3.7 %field_inside.1.sums_in = f32[72,128]{1,0:T(8,128)S(1)} custom-call(f32[64,128]{1,0:T(8,128)S(1)} %copy-done, f32[32,128]{1,0:T(8,128)S(1)} %collective-permute-done.refs_1_, f32[96,128]{1,0:T(8,128)S(1)} %collective-permute-done.1.refs_2_, f32[32,128]{1,0:T(8,128)S(1)} %get-tuple-element.32.own_speed.refs_3_.speed, ...), custom_call_target="tpu_custom_call" | custom-call | flops 2147483648 | bytes 1048576 | tf_op jit(solution)/shard_map/field_inside/pallas_call | solution.py:667
  29.5 0.1 collective-permute-done.8.far_speed
  29.6 0.2 collective-permute-done.7.near_speed
  29.9 2.0 %field_outside.1 = (f32[24,128]{1,0:T(8,128)S(1)}, f32[16,128]{1,0:T(8,128)S(1)}) custom-call(f32[64,128]{1,0:T(8,128)S(1)} %copy-done, f32[32,128]{1,0:T(8,128)S(1)} %get-tuple-element.32.own_speed.refs_3_.speed, f32[72,128]{1,0:T(8,128)S(1)} %field_inside.1.sums_in, f32[96,128]{1,0:T(8,128)S(1)} %collective-permute-done.2.near.near_old, ...), custom_call_target="tpu_custom_call" | custom-call | flops 1073741824 | bytes 1048576 | tf_op jit(solution)/shard_map/field_outside/pallas_call | solution.py:667
  31.8 0.0 collective-permute-start.11
  31.8 0.4 collective-permute-start.10
  32.2 1.6 %collective-permute-start.9 = (f32[16,128]{1,0:T(8,128)S(1)}, f32[16,128]{1,0:T(8,128)S(1)}, u32[]{:S(2)}, u32[]{:S(2)}) collective-permute-start(f32[16,128]{1,0:T(8,128)S(1)} %get-tuple-element.44), channel_id=1, source_target_pairs={{0,1},{1,0},{2,3},{3,2},{4,5},{5,4},{6,7},{7,6},{8,9},{9,8},{10,11... | collective-permute-start | bytes 24584 | tf_op jit(solution)/shard_map/ppermute | solution.py:646
  33.8 1.2 %collective-permute-done.11 = f32[16,128]{1,0:T(8,128)S(1)} collective-permute-done((f32[16,128]{1,0:T(8,128)S(1)}, f32[16,128]{1,0:T(8,128)S(1)}, u32[]{:S(2)}, u32[]{:S(2)}) %collective-permute-start.11) | collective-permute-done | bytes 8224 | tf_op jit(solution)/shard_map/ppermute | solution.py:646
  35.0 0.6 %collective-permute-done.10 = f32[16,128]{1,0:T(8,128)S(1)} collective-permute-done((f32[16,128]{1,0:T(8,128)S(1)}, f32[16,128]{1,0:T(8,128)S(1)}, u32[]{:S(2)}, u32[]{:S(2)}) %collective-permute-start.10) | collective-permute-done | bytes 8224 | tf_op jit(solution)/shard_map/ppermute | solution.py:646
  35.6 0.0 collective-permute-done.9
  35.6 9.0 %all_to_all.5.parts = f32[4,16,128]{2,1,0:T(8,128)S(1)} all-to-all(f32[4,16,128]{2,1,0:T(8,128)S(1)} %broadcast_in_dim.3), channel_id=1, replica_groups=mesh['groups'=2,'down'=4,'cross'=2,'depth'=2] {'down'}, dimensions={0} | all-to-all | bytes 65536 | tf_op jit(solution)/shard_map/all_to_all | solution.py:730
  44.6 0.9 %library.1 = (f32[3,2,2,2,128]{4,3,2,1,0:T(2,128)}, f32[3,2,2,2,128]{4,3,2,1,0:T(2,128)}, f32[2,2,2]{2,1,0:T(2,128)}, f32[48,48]{1,0:T(8,128)}, f32[1,48]{1,0:T(1,128)}) custom-call(f32[1,48]{1,0:T(1,128)S(1)} %get-tuple-element.37.coefficients, f32[4,16,128]{2,1,0:T(8,128)S(1)} %all_to_all.5.parts, f32[32,128]{1,0:T(8,128)S(1)} %get-tuple-element.32.own_speed.refs_3_.speed, ...), custom_call_target="tpu_custom_call" | custom-call | tf_op jit(solution)/shard_map/library/pallas_call | solution.py:731
  (21 shorter events, 0.1 us)
Async XLA Ops:
  2.0 1.6 %collective-permute-start = (f32[32,128]{1,0:T(8,128)}, f32[32,128]{1,0:T(8,128)S(1)}, u32[]{:S(2)}, u32[]{:S(2)}) collective-permute-start(f32[32,128]{1,0:T(8,128)} %get-tuple-element.29), channel_id=1, source_target_pairs={{0,1},{1,0},{2,3},{3,2},{4,5},{5,4},{6,7},{7,6},{8,9},{9,8},{10,11... | collective-permute-start | bytes 49160 | tf_op jit(solution)/shard_map/ppermute | solution.py:577
  2.6 1.1 %copy-start = (f32[64,128]{1,0:T(8,128)S(1)}, f32[64,128]{1,0:T(8,128)}, u32[]{:S(2)}) copy-start(f32[64,128]{1,0:T(8,128)} %get-tuple-element.28.refs_0_.own) | copy-start | bytes 98308
  3.6 5.0 %collective-permute-start.1 = (f32[96,128]{1,0:T(8,128)S(1)}, f32[96,128]{1,0:T(8,128)S(1)}, u32[]{:S(2)}, u32[]{:S(2)}) collective-permute-start(f32[96,128]{1,0:T(8,128)S(1)} %pad_maximum_fusion), channel_id=1, source_target_pairs={{0,2},{2,0},{1,3},{3,1},{4,6},{6,4},{5,7},{7,5},{8,10},{10,8},{9,1... | collective-permute-start | bytes 147464 | tf_op jit(solution)/shard_map/ppermute | solution.py:580
  8.6 7.5 %collective-permute-start.3 = (f32[96,128]{1,0:T(8,128)S(1)}, f32[96,128]{1,0:T(8,128)S(1)}, u32[]{:S(2)}, u32[]{:S(2)}) collective-permute-start(f32[96,128]{1,0:T(8,128)S(1)} %get-tuple-element.51), channel_id=1, source_target_pairs={{0,12},{4,8},{8,4},{12,0},{1,13},{5,9},{9,5},{13,1},{2,14},{6,10},... | collective-permute-start | bytes 147464 | tf_op jit(solution)/shard_map/ppermute | solution.py:632
  12.8 4.1 %collective-permute-start.2 = (f32[96,128]{1,0:T(8,128)S(1)}, f32[96,128]{1,0:T(8,128)S(1)}, u32[]{:S(2)}, u32[]{:S(2)}) collective-permute-start(f32[96,128]{1,0:T(8,128)S(1)} %get-tuple-element.52), channel_id=1, source_target_pairs={{0,4},{4,0},{8,12},{12,8},{1,5},{5,1},{9,13},{13,9},{2,6},{6,2},{1... | collective-permute-start | bytes 147464 | tf_op jit(solution)/shard_map/ppermute | solution.py:631
  18.5 3.2 %collective-permute-start.6 = (f32[16,128]{1,0:T(8,128)S(1)}, f32[16,128]{1,0:T(8,128)S(1)}, u32[]{:S(2)}, u32[]{:S(2)}) collective-permute-start(f32[16,128]{1,0:T(8,128)S(1)} %get-tuple-element.31), channel_id=1, source_target_pairs={{0,3},{1,2},{2,1},{3,0},{4,7},{5,6},{6,5},{7,4},{8,11},{9,10},{10,... | collective-permute-start | bytes 24584 | tf_op jit(solution)/shard_map/ppermute | solution.py:586
  18.5 2.4 %collective-permute-start.4 = (f32[16,128]{1,0:T(8,128)S(1)}, f32[16,128]{1,0:T(8,128)S(1)}, u32[]{:S(2)}, u32[]{:S(2)}) collective-permute-start(f32[16,128]{1,0:T(8,128)S(1)} %get-tuple-element.31), channel_id=1, source_target_pairs={{0,1},{1,0},{2,3},{3,2},{4,5},{5,4},{6,7},{7,6},{8,9},{9,8},{10,11... | collective-permute-start | bytes 24584 | tf_op jit(solution)/shard_map/ppermute | solution.py:577
  20.1 3.7 %collective-permute-start.5 = (f32[32,128]{1,0:T(8,128)S(1)}, f32[32,128]{1,0:T(8,128)S(1)}, u32[]{:S(2)}, u32[]{:S(2)}) collective-permute-start(f32[32,128]{1,0:T(8,128)S(1)} %get-tuple-element.32.own_speed.refs_3_.speed), channel_id=1, source_target_pairs={{0,2},{2,0},{1,3},{3,1},{4,6},{6,4},{5,7},{7,5},{8,10},{10,8},{9,1... | collective-permute-start | bytes 49160 | tf_op jit(solution)/shard_map/ppermute | solution.py:576
  21.6 0.7 %copy-start.1 = (f32[48]{0:T(128)S(1)}, f32[48]{0:T(128)}, u32[]{:S(2)}) copy-start(f32[48]{0:T(128)} %param.9) | copy-start | bytes 580
  23.9 5.7 %collective-permute-start.8 = (f32[48,128]{1,0:T(8,128)S(1)}, f32[48,128]{1,0:T(8,128)S(1)}, u32[]{:S(2)}, u32[]{:S(2)}) collective-permute-start(f32[48,128]{1,0:T(8,128)S(1)} %get-tuple-element.53), channel_id=1, source_target_pairs={{0,12},{4,8},{8,4},{12,0},{1,13},{5,9},{9,5},{13,1},{2,14},{6,10},... | collective-permute-start | bytes 73736 | tf_op jit(solution)/shard_map/ppermute | solution.py:632
  25.8 4.1 %collective-permute-start.7 = (f32[48,128]{1,0:T(8,128)S(1)}, f32[48,128]{1,0:T(8,128)S(1)}, u32[]{:S(2)}, u32[]{:S(2)}) collective-permute-start(f32[48,128]{1,0:T(8,128)S(1)} %get-tuple-element.54), channel_id=1, source_target_pairs={{0,4},{4,0},{8,12},{12,8},{1,5},{5,1},{9,13},{13,9},{2,6},{6,2},{1... | collective-permute-start | bytes 73736 | tf_op jit(solution)/shard_map/ppermute | solution.py:631
  31.8 3.1 %collective-permute-start.11 = (f32[16,128]{1,0:T(8,128)S(1)}, f32[16,128]{1,0:T(8,128)S(1)}, u32[]{:S(2)}, u32[]{:S(2)}) collective-permute-start(f32[16,128]{1,0:T(8,128)S(1)} %get-tuple-element.44), channel_id=1, source_target_pairs={{0,3},{1,2},{2,1},{3,0},{4,7},{5,6},{6,5},{7,4},{8,11},{9,10},{10,... | collective-permute-start | bytes 24584 | tf_op jit(solution)/shard_map/ppermute | solution.py:646
  31.8 3.7 %collective-permute-start.10 = (f32[16,128]{1,0:T(8,128)S(1)}, f32[16,128]{1,0:T(8,128)S(1)}, u32[]{:S(2)}, u32[]{:S(2)}) collective-permute-start(f32[16,128]{1,0:T(8,128)S(1)} %get-tuple-element.44), channel_id=1, source_target_pairs={{0,2},{1,3},{2,0},{3,1},{4,6},{5,7},{6,4},{7,5},{8,10},{9,11},{10,... | collective-permute-start | bytes 24584 | tf_op jit(solution)/shard_map/ppermute | solution.py:646
  32.2 3.4 %collective-permute-start.9 = (f32[16,128]{1,0:T(8,128)S(1)}, f32[16,128]{1,0:T(8,128)S(1)}, u32[]{:S(2)}, u32[]{:S(2)}) collective-permute-start(f32[16,128]{1,0:T(8,128)S(1)} %get-tuple-element.44), channel_id=1, source_target_pairs={{0,1},{1,0},{2,3},{3,2},{4,5},{5,4},{6,7},{7,6},{8,9},{9,8},{10,11... | collective-permute-start | bytes 24584 | tf_op jit(solution)/shard_map/ppermute | solution.py:646
